TPU v7x, 32 devices: a whole 2x2x4 slice. The times are simulated.
32 devices in a mesh: groups: 2 (over x), seq: 16 (over z, y, core).
Axes of the slice: x: 2, y: 2, z: 4, core: 2. Of those that a mesh axis runs over, the one named last changes fastest.
Arguments:
- tokens: bfloat16 [8192, 2048], P(('groups', 'seq')), parts along dimension 0, may hold values from -60 to 60
- w_query: bfloat16 [2048, 1024], P('seq'), may hold values from -0.125 to 0.125
- w_keyval: bfloat16 [2048, 2048], P('seq'), may hold values from -0.125 to 0.125
- global_off: int32 [32], P(('groups', 'seq')), parts along dimension 0, may hold values from 0 to 255
- rand_dev: int32 [128, 8, 3], P('groups'), parts along dimension 0, may hold values from 0 to 15, all different within a row; in each aligned block of 32 rows (0 to 31, 32 to 63, ..., all dimensions but the last counted through in order) at most 9 rows name the same one
- rand_sub: int32 [128, 8, 3], P('groups'), parts along dimension 0, may hold values from 0 to 3
Outputs:
- context: bfloat16 [8192, 1024], P(('groups', 'seq')), parts along dimension 0
There are 2 independent parts, one for each index of `groups`. A program takes and returns all parts, laid end to end along the dimension named above; an argument that names none is the same for every part. Nothing has to cross between parts.
Inputs may be any that keep to these rules, and one draw needn't show every extreme that they name: Over the 4 query blocks of one shard and all heads, no shard is named by more than 9 entries of rand_dev, and this bound is reached in every draw; the 3 entries of one query block and head name different shards.
All inputs are finite; a program needn't handle non-finite values.
Results may differ from a plain program's by a relative error of at most 0.0045.
The roundings to bfloat16 on the way count: a program that leaves them out, or rounds other values in their place, can miss the bound.
Values may be sent and summed in bfloat16 or wider, within the bound.
A program may use at most 128 MiB of HBM per device.

v0:
```python
import jax
import jax.numpy as jnp
from jax import lax
from jax.sharding import PartitionSpec as P

H = 8
HD = 128
BLOCK = 64
R = 3
BLK_DEV = 4


def padded_2(block, sides, width):
    for axis, dim in sides:
        count = lax.axis_size(axis)
        forward = [(i, i + 1) for i in range(count - 1)]
        backward = [(target, source) for source, target in forward]
        low = lax.ppermute(
            lax.slice_in_dim(block, block.shape[dim] - width, None, axis=dim), axis, forward
        )
        high = lax.ppermute(lax.slice_in_dim(block, 0, width, axis=dim), axis, backward)
        block = jnp.concatenate([low, block, high], axis=dim)
    return block


def fold_rows(left, piece):
    return jnp.dot(left, piece, preferred_element_type=jnp.float32)


def local(tokens, w_query, w_keyval, global_off, rand_dev, rand_sub):
    ntok = tokens.shape[0]
    nseq = lax.axis_size("seq")
    me_index = lax.axis_index("seq")
    nblk = ntok // BLOCK
    inner = H * HD
    glob_rows = lax.all_gather(jnp.take(tokens, global_off, axis=0), "seq", axis=0, tiled=True)
    left_kv = jnp.concatenate([tokens, glob_rows], axis=0)
    query = fold_rows(tokens, lax.all_gather(w_query, "seq", axis=0, tiled=True))
    keyval = fold_rows(left_kv, lax.all_gather(w_keyval, "seq", axis=0, tiled=True))
    query = query.astype(jnp.bfloat16)
    keyval = keyval.astype(jnp.bfloat16)
    glob_kv = keyval[ntok:]
    keyval = keyval[:ntok]
    glob_kv = glob_kv.reshape(glob_kv.shape[0], 2, H, HD)
    padded = padded_2(keyval, (("seq", 0),), BLOCK)
    window = jnp.concatenate(
        [padded[j * BLOCK : j * BLOCK + ntok].reshape(nblk, BLOCK, 2, H, HD) for j in range(3)],
        axis=1,
    )
    capacity = max(2, 3 * BLK_DEV * H * R // (2 * nseq))
    nreq = nblk * H * R
    dev_all = rand_dev.reshape(nseq, nreq)
    sub_all = rand_sub.reshape(nseq, nreq)
    match = (dev_all == me_index).astype(jnp.int32)
    slot_all = jnp.cumsum(match, axis=1) - 1
    head_of = jnp.arange(nreq, dtype=jnp.int32) // R % H
    code_all = head_of[None, :] * nblk + sub_all
    picked = (match[:, None, :] == 1) & (
        slot_all[:, None, :] == jnp.arange(capacity, dtype=jnp.int32)[None, :, None]
    )
    source = jnp.sum(jnp.where(picked, code_all[:, None, :], 0), axis=2)
    tiles = (
        keyval.reshape(nblk, BLOCK, 2, H, HD)
        .transpose(3, 0, 1, 2, 4)
        .reshape(H * nblk, BLOCK, 2 * HD)
    )
    outgoing = jnp.take(tiles, source, axis=0)
    incoming = lax.all_to_all(outgoing, "seq", split_axis=0, concat_axis=0, tiled=True)
    my_dev = lax.dynamic_slice_in_dim(rand_dev, me_index * nblk, nblk, 0).reshape(nreq)
    onehot = (my_dev[:, None] == jnp.arange(nseq, dtype=jnp.int32)[None, :]).astype(jnp.int32)
    my_slot = jnp.sum(onehot * (jnp.cumsum(onehot, axis=0) - 1), axis=1)
    flat_index = my_dev * capacity + my_slot
    fetched = jnp.take(incoming.reshape(nseq * capacity, BLOCK, 2 * HD), flat_index, axis=0)
    fetched = fetched.reshape(nblk, H, R, BLOCK, 2, HD)
    scale = HD ** (-0.5)
    qry = query.reshape(nblk, BLOCK, H, HD)
    s_win = (
        jnp.einsum("bqhd,bkhd->bhqk", qry, window[:, :, 0], preferred_element_type=jnp.float32)
        * scale
    )
    s_rnd = (
        jnp.einsum(
            "bqhd,bhrkd->bhqrk", qry, fetched[:, :, :, :, 0], preferred_element_type=jnp.float32
        ).reshape(nblk, H, BLOCK, R * BLOCK)
        * scale
    )
    s_glb = (
        jnp.einsum("bqhd,ghd->bhqg", qry, glob_kv[:, 0], preferred_element_type=jnp.float32) * scale
    )
    blk_ids = me_index * nblk + jnp.arange(nblk, dtype=jnp.int32)
    left_ok = jnp.repeat((blk_ids > 0)[:, None], BLOCK, axis=1)
    right_ok = jnp.repeat((blk_ids < nseq * nblk - 1)[:, None], BLOCK, axis=1)
    middle_ok = jnp.ones((nblk, BLOCK), dtype=bool)
    window_ok = jnp.concatenate([left_ok, middle_ok, right_ok], axis=1)
    s_win = jnp.where(window_ok[:, None, None, :], s_win, -jnp.inf)
    scores = jnp.concatenate([s_win, s_rnd, s_glb], axis=3)
    highest = jnp.max(scores, axis=3, keepdims=True)
    expo = jnp.exp(scores - highest)
    weights = (expo / jnp.sum(expo, axis=3, keepdims=True)).astype(jnp.bfloat16)
    w_win = weights[..., : 3 * BLOCK]
    w_rnd = weights[..., 3 * BLOCK : 3 * BLOCK + R * BLOCK].reshape(nblk, H, BLOCK, R, BLOCK)
    w_glb = weights[..., 3 * BLOCK + R * BLOCK :]
    ctx = jnp.einsum("bhqk,bkhd->bqhd", w_win, window[:, :, 1], preferred_element_type=jnp.float32)
    ctx = ctx + jnp.einsum(
        "bhqrk,bhrkd->bqhd", w_rnd, fetched[:, :, :, :, 1], preferred_element_type=jnp.float32
    )
    ctx = ctx + jnp.einsum(
        "bhqg,ghd->bqhd", w_glb, glob_kv[:, 1], preferred_element_type=jnp.float32
    )
    return ctx.reshape(ntok, inner).astype(jnp.bfloat16)


def solution(mesh):
    in_specs = (
        P(("groups", "seq"), None),
        P("seq", None),
        P("seq", None),
        P(("groups", "seq")),
        P("groups", None, None),
        P("groups", None, None),
    )
    out_specs = P(("groups", "seq"), None)
    return jax.shard_map(local, mesh=mesh, in_specs=in_specs, out_specs=out_specs, check_vma=False)
```

profile of v0, /device:TPU:13, one launch (start us, length us, event | category | flops | bytes accessed | tf_op | source)
XLA Modules:
  0.0 279.5 jit_solution(17051422874582534580)
XLA Ops:
  6.5 0.7 all-gather.4.cloned.1.call-update
  7.3 0.7 all-gather.6.cloned.1.call-update
  8.7 0.9 copy.149
  9.6 0.2 reshape.195
  9.7 0.7 compare_convert_fusion
  10.4 0.2 copy.148
  10.6 0.2 reshape.219
  10.8 0.3 reduce_window_sum.23
  11.1 0.8 fusion.23
  11.8 16.2 %all-gather = bf16[16,1,2048]{2,1,0:T(2,128)(2,1)S(1)} all-gather(bf16[1,1,2048]{2,1,0:T(2,128)(2,1)S(1)} %fusion.23), channel_id=1, replica_groups=mesh['groups'=2,'seq'=16] {'seq'}, dimensions={0}, use_global_device_ids=true | all-gather | bytes 69632 | tf_op jit(solution)/shard_map/all_gather | solution.py:36
  28.1 0.2 select_reduce_fusion
  28.3 0.1 copy.152
  28.4 0.1 reshape.229
  28.5 0.1 copy.150
  28.6 56.3 %all-gather.4.cloned.1.call-done = bf16[2048,2048]{1,0:T(8,128)(2,1)} async-done(((bf16[128,2048]{1,0:T(8,128)(2,1)}), bf16[2048,2048]{1,0:T(8,128)(2,1)}) %all-gather.4.cloned.1.call-update) | async-done | bytes 8388624 | tf_op jit(solution)/shard_map/all_gather | solution.py:39
  84.9 6.2 %convolution_convert_fusion = bf16[272,2048]{1,0:T(8,128)(2,1)S(1)} fusion(bf16[2048,2048]{1,0:T(8,128)(2,1)} %all-gather.4.cloned.1.call-done, bf16[16,2048]{1,0:T(8,128)(2,1)S(1)} %bitcast.117, bf16[256,2048]{1,0:T(8,128)(2,1)} %param.6), kind=kOutput, calls=%fused_computation.7 | convolution fusion | flops 2284486656 | bytes 10616832 | tf_op jit(solution)/shard_map/dot_general | solution.py:27
  91.1 0.3 slice_bitcast_fusion.15
  91.4 0.2 copy.178
  91.7 2.1 copy.208
  93.7 1.8 reshape.196
  95.5 7.6 %gather_fusion = bf16[144,64,256]{2,1,0:T(8,128)(2,1)} fusion(bf16[32,64,256]{2,1,0:T(8,128)(2,1)S(1)} %reshape.196, s32[1024]{0:T(1024)S(1)} %pad_clamp_fusion.1), kind=kCustom, calls=%fused_computation | custom fusion | bytes 9437760 | tf_op jit(solution)/shard_map/jit(_take)/gather | solution.py:67
  103.0 5.0 %broadcast_select_fusion = bf16[16,9,64,256]{3,2,1,0:T(8,128)(2,1)} fusion(bf16[16,9,64,256]{3,2,1,0:T(8,128)(2,1)} %bitcast.104, pred[16,9]{1,0:T(8,128)(4,1)S(1)} %copy.150), kind=kLoop, calls=%fused_computation.2 | loop fusion | flops 2359296 | bytes 9437328 | tf_op jit(solution)/shard_map/jit(_take)/select_n | solution.py:67
  108.0 6.4 %all-to-all-start = ((bf16[16,9,64,256]{3,2,1,0:T(8,128)(2,1)}), bf16[16,9,64,256]{3,2,1,0:T(8,128)(2,1)}, u32[]{:S(2)}, u32[]{:S(2)}) async-start(bf16[16,9,64,256]{3,2,1,0:T(8,128)(2,1)} %broadcast_select_fusion), calls=%async_computation | async-start | bytes 9437184 | tf_op jit(solution)/shard_map/all_to_all | solution.py:68
  114.5 0.1 copy.173
  114.6 0.1 reshape.194
  114.8 0.1 mul.63
  114.9 0.1 fusion.22
  115.0 0.1 reduce_window_sum.22
  115.1 0.2 select_reduce_fusion.1
  115.3 0.1 reduce_sum.34
  115.4 0.1 pad.12.clone
  115.7 49.7 %all-gather.6.cloned.1.call-done = bf16[2048,1024]{1,0:T(8,128)(2,1)} async-done(((bf16[128,1024]{1,0:T(8,128)(2,1)}), bf16[2048,1024]{1,0:T(8,128)(2,1)}) %all-gather.6.cloned.1.call-update) | async-done | bytes 4194320 | tf_op jit(solution)/shard_map/all_gather | solution.py:38
  165.3 3.8 %fusion.9 = bf16[32,8,8,128]{3,1,2,0:T(8,128)(2,1)S(1)} fusion(bf16[256,2048]{1,0:T(8,128)(2,1)} %param.6, bf16[2048,1024]{1,0:T(8,128)(2,1)} %all-gather.6.cloned.1.call-done), kind=kOutput, calls=%fused_computation.24 | convolution fusion | flops 1074003968 | bytes 5767168 | tf_op jit(solution)/shard_map/dot_general | solution.py:27
  169.2 0.1 copy.176
  169.3 0.8 bitcast_bitcast_fusion
  170.2 0.8 fusion.30
  171.0 2.7 collective-permute-start.1
  173.7 3.9 %collective-permute-start = (bf16[64,2048]{1,0:T(8,128)(2,1)}, bf16[64,2048]{1,0:T(8,128)(2,1)S(1)}, u32[]{:S(2)}, u32[]{:S(2)}) collective-permute-start(bf16[64,2048]{1,0:T(8,128)(2,1)} %get-tuple-element.17), channel_id=1, source_target_pairs={{0,1},{1,2},{2,3},{3,4},{4,5},{5,6},{6,7},{7,8},{8,9},{9,10},{10,1... | collective-permute-start | bytes 786440 | tf_op jit(solution)/shard_map/ppermute | solution.py:18
  177.6 0.5 fusion.32
  178.2 1.4 copy.158
  179.5 56.4 %collective-permute-done.1 = bf16[64,2048]{1,0:T(8,128)(2,1)S(1)} collective-permute-done((bf16[64,2048]{1,0:T(8,128)(2,1)}, bf16[64,2048]{1,0:T(8,128)(2,1)S(1)}, u32[]{:S(2)}, u32[]{:S(2)}) %collective-permute-start.1) | collective-permute-done | bytes 262176 | tf_op jit(solution)/shard_map/ppermute | solution.py:21
  235.9 0.4 fusion.15
  236.3 0.2 copy.177
  236.5 0.2 copy.179
  236.8 0.3 copy_dynamic-update-slice_fusion.2
  237.1 0.3 copy_dynamic-update-slice_fusion.1
  237.4 0.3 copy_dynamic-update-slice_fusion
  237.8 1.6 copy-done.8
  239.4 2.5 fusion.33
  241.9 3.1 %gather_fusion.1 = bf16[96,64,256]{2,1,0:T(8,128)(2,1)S(1)} fusion(bf16[144,64,256]{2,1,0:T(8,128)(2,1)} %bitcast.9, s32[1024]{0:T(1024)S(1)} %pad_clamp_fusion), kind=kCustom, calls=%fused_computation.1 | custom fusion | bytes 6291840 | tf_op jit(solution)/shard_map/jit(_take)/gather | solution.py:73
  245.0 3.0 %gather.17 = bf16[4,8,3,64,2,128]{5,4,3,2,1,0:T(2,128)(2,1)} reshape(bf16[96,64,256]{2,1,0:T(8,128)(2,1)S(1)} %gather_fusion.1) | data formatting | bytes 6291456 | tf_op jit(solution)/shard_map/jit(_take)/gather | solution.py:73
  248.0 2.4 copy_select_fusion
  250.5 2.6 fusion.34
  253.1 2.7 copy.157
  255.9 3.4 %fusion.1 = f32[4,8,64]{2,1,0:T(8,128)S(1)} fusion(f32[4,8,64]{2,1,0:T(8,128)S(1)} %copy_maximum_fusion, f32[4,8,64,16]{3,2,1,0:T(8,128)S(1)} %copy-done.4, f32[4,8,64,192]{3,2,1,0:T(8,128)S(1)} %copy.157, f32[4,8,64,192]{3,2,1,0:T(8,128)} %get-tuple-element.27), kind=kLoop, calls=%fused_computation.9 | loop fusion | flops 3274752 | bytes 3293184 | tf_op jit(solution)/shard_map/reduce_sum | solution.py:99
  259.3 2.2 divide_convert_fusion
  261.5 1.3 copy-done.2
  262.8 1.4 slice.85
  264.2 2.5 copy.160
  266.8 2.2 fusion.4
  269.0 2.1 fusion.7
  271.1 0.3 fusion.8
  271.4 0.3 copy.164
  271.7 0.9 copy.209
  (45 shorter events, 0.5 us)
Async XLA Ops:
  6.5 78.4 %all-gather.4.cloned.1.call-start = ((), (), s32[]{:S(2)}) async-start(), calls=%async_computation.1 | async-start | bytes 8912896 | tf_op jit(solution)/shard_map/all_gather | solution.py:39
  7.3 158.1 %all-gather.6.cloned.1.call-start = ((), (), s32[]{:S(2)}) async-start(), calls=%async_computation.2 | async-start | bytes 4456448 | tf_op jit(solution)/shard_map/all_gather | solution.py:38
  91.1 2.6 copy-start.6
  108.0 6.4 %copy-start.10 = (s32[64,8,3]{0,1,2:T(8,128)S(1)}, s32[64,8,3]{0,1,2:T(8,128)}, u32[]{:S(2)}) copy-start(s32[64,8,3]{0,1,2:T(8,128)} %param.10) | copy-start | bytes 18436
  108.0 133.8 %all-to-all-start = ((bf16[16,9,64,256]{3,2,1,0:T(8,128)(2,1)}), bf16[16,9,64,256]{3,2,1,0:T(8,128)(2,1)}, u32[]{:S(2)}, u32[]{:S(2)}) async-start(bf16[16,9,64,256]{3,2,1,0:T(8,128)(2,1)} %broadcast_select_fusion), calls=%async_computation | async-start | bytes 9437184 | tf_op jit(solution)/shard_map/all_to_all | solution.py:68
  165.3 4.8 %copy-start.7 = (bf16[272,2048]{1,0:T(8,128)(2,1)S(1)}, bf16[272,2048]{1,0:T(8,128)(2,1)}, u32[]{:S(2)}) copy-start(bf16[272,2048]{1,0:T(8,128)(2,1)} %copy-done.6) | copy-start | bytes 3342340
  171.0 64.9 %collective-permute-start.1 = (bf16[64,2048]{1,0:T(8,128)(2,1)}, bf16[64,2048]{1,0:T(8,128)(2,1)S(1)}, u32[]{:S(2)}, u32[]{:S(2)}) collective-permute-start(bf16[64,2048]{1,0:T(8,128)(2,1)} %get-tuple-element.16), channel_id=1, source_target_pairs={{1,0},{2,1},{3,2},{4,3},{5,4},{6,5},{7,6},{8,7},{9,8},{10,9},{11,1... | collective-permute-start | bytes 786440 | tf_op jit(solution)/shard_map/ppermute | solution.py:21
  173.7 62.2 %collective-permute-start = (bf16[64,2048]{1,0:T(8,128)(2,1)}, bf16[64,2048]{1,0:T(8,128)(2,1)S(1)}, u32[]{:S(2)}, u32[]{:S(2)}) collective-permute-start(bf16[64,2048]{1,0:T(8,128)(2,1)} %get-tuple-element.17), channel_id=1, source_target_pairs={{0,1},{1,2},{2,3},{3,4},{4,5},{5,6},{6,7},{7,8},{8,9},{9,10},{10,1... | collective-permute-start | bytes 786440 | tf_op jit(solution)/shard_map/ppermute | solution.py:18
  237.8 1.7 copy-start.8
  248.0 2.4 copy-start.9
  250.5 2.7 copy-start
  253.1 2.8 copy-start.4
  255.8 3.4 %copy-start.5 = (f32[4,8,64,192]{3,2,1,0:T(8,128)S(1)}, f32[4,8,64,192]{3,2,1,0:T(8,128)}, u32[]{:S(2)}) copy-start(f32[4,8,64,192]{3,2,1,0:T(8,128)} %get-tuple-element.27) | copy-start | bytes 4718596
  261.5 1.3 copy-start.2
  262.8 3.9 %copy-start.1 = (bf16[4,8,3,64,2,128]{5,3,2,1,0,4:T(8,128)(2,1)S(1)}, bf16[4,8,3,64,2,128]{5,3,2,1,0,4:T(8,128)(2,1)}, u32[]{:S(2)}) copy-start(bf16[4,8,3,64,2,128]{5,3,2,1,0,4:T(8,128)(2,1)} %copy-done) | copy-start | bytes 9437188
  266.8 2.2 copy-start.3
Sparse Core Ops, SparseCore 0:
  9.5 75.3 all-gather.3
  87.1 78.2 all-gather.5
where the time goes:
time: 280 us; the launch traced here: 279 us
  waiting for transfers between devices  164 us (59%)
  local copies, waits for them, and re-layouts  36 us (13%)
  matrix products  20.2 us (7%)
  blocking collectives  16.2 us (6%)
  other arithmetic  15.8 us (6%)
  between operations  14.5 us (5%)
  starting transfers between devices  13.1 us (5%)
    ppermute x1, waiting for transfers between devices, padded_2(): lax.ppermute(lax.slice_in_dim(block, 0, width, axis=dim), axis, backward)  56.4 us
    all_gather x1, waiting for transfers between devices, local(): lax.all_gather(w_keyval, 'seq', axis=0, tiled=True)  56.3 us
    all_gather x1, waiting for transfers between devices, local(): lax.all_gather(w_query, 'seq', axis=0, tiled=True)  49.7 us
    all_gather x1, blocking collectives, local(): lax.all_gather(jnp.take(tokens, global_off, axis=0), 'seq', axis=0, tiled...  16.2 us
    dot_general x2, matrix products, fold_rows(): return jnp.dot(left, piece, preferred_element_type=jnp.float32)  10 us
    gather x1, local copies, waits for them, and re-layouts, local(): outgoing = jnp.take(tiles, source, axis=0)  7.55 us
    unnamed x35, local copies, waits for them, and re-layouts  6.74 us
    all_to_all x1, starting transfers between devices, local(): lax.all_to_all(outgoing, 'seq', split_axis=0, concat_axis=0, tiled=True)  6.39 us
  transfers between devices with their start and end apart: 5, of which 3 were waited for; matrix products, arithmetic and copies ran while one was open for 14% of the time, Pallas kernels for 0%

commit v1 on v0

--- a/solution.py
+++ b/solution.py
@@ -1,6 +1,10 @@
+import functools
+
 import jax
 import jax.numpy as jnp
 from jax import lax
+from jax.experimental import pallas as pl
+from jax.experimental.pallas import tpu as pltpu
 from jax.sharding import PartitionSpec as P
 
 H = 8
@@ -8,6 +12,8 @@
 BLOCK = 64
 R = 3
 BLK_DEV = 4
+LANES = 4
+MESH = pl.DeviceIdType.MESH
 
 
 def padded_2(block, sides, width):
@@ -110,6 +116,346 @@
     return ctx.reshape(ntok, inner).astype(jnp.bfloat16)
 
 
+def fused_kernel(
+    planes, tok_hbm, wq_hbm, wkv_hbm, off_ref, blocks_ref, out_ref,
+    tok, wts, qry, kv, events, ctx,
+    local_sem, w_send, w_recv, wx_send, wx_recv, wl_send, wl_recv,
+    t_send, t_recv, k_send, k_recv, e_send, e_recv, c_send, c_recv,
+):
+    ntok = tok_hbm.shape[0]
+    slot_rows = tok.shape[1]
+    extra = slot_rows - ntok
+    nblk = ntok // BLOCK
+    heads = H // planes
+    cols = heads * HD
+    half = wts.shape[3]
+    x = lax.axis_index("groups")
+    me = lax.axis_index("seq")
+    z = me // LANES
+    lane = me % LANES
+    core_lane = lane + 1 - 2 * (lane % 2)
+    y_lane = (lane + 2) % LANES
+    diag_lane = (core_lane + 2) % LANES
+
+    def at(plane, where):
+        return {"seq": plane * LANES + where}
+
+    x_peer = {"groups": 1 - x}
+    core_peer = at(z, core_lane)
+    y_peer = at(z, y_lane)
+    diag_peer = at(z, diag_lane)
+
+    def remote(src, dst, send, recv, peer):
+        return pltpu.make_async_remote_copy(
+            src_ref=src, dst_ref=dst, send_sem=send, recv_sem=recv, device_id=peer,
+            device_id_type=MESH,
+        )
+
+    own_tok = pltpu.make_async_copy(tok_hbm, tok.at[z, pl.ds(0, ntok)], local_sem.at[0])
+    own_tok.start()
+
+    def weight_parts(plane):
+        rows = pl.ds(pl.multiple_of(x * half, half), half)
+        start = pl.multiple_of(plane * cols, cols)
+        return (
+            wq_hbm.at[rows, pl.ds(start, cols)],
+            wkv_hbm.at[rows, pl.ds(start, cols)],
+            wkv_hbm.at[rows, pl.ds(pl.multiple_of(H * HD + plane * cols, cols), cols)],
+        )
+
+    own_w = []
+    for part, src in enumerate(weight_parts(z)):
+        copy = pltpu.make_async_copy(
+            src, wts.at[z, lane, x, :, pl.ds(part * cols, cols)], local_sem.at[1 + part]
+        )
+        copy.start()
+        own_w.append(copy)
+
+    barrier = pltpu.get_barrier_semaphore()
+    for step in range(1, planes):
+        pl.semaphore_signal(
+            barrier, inc=1, device_id=at((z + step) % planes, lane), device_id_type=MESH
+        )
+    for peer in (x_peer, core_peer, y_peer, diag_peer):
+        pl.semaphore_signal(barrier, inc=1, device_id=peer, device_id_type=MESH)
+    pl.semaphore_wait(barrier, planes - 1 + 4)
+
+    def weight_copy(step, part):
+        plane = (z + step) % planes
+        return remote(
+            weight_parts(plane)[part],
+            wts.at[z, lane, x, :, pl.ds(part * cols, cols)],
+            w_send.at[step - 1, part], w_recv.at[step - 1, part], at(plane, lane),
+        )
+
+    def weight_landed(step, part):
+        plane = (z + planes - step) % planes
+        here = wts.at[plane, lane, x, :, pl.ds(part * cols, cols)]
+        return remote(here, here, w_send.at[step - 1, part], w_recv.at[step - 1, part], at(plane, lane))
+
+    for step in range(1, planes):
+        for part in range(3):
+            weight_copy(step, part).start()
+
+    own_tok.wait()
+    spot = lax.broadcasted_iota(jnp.int32, (extra, ntok), 0) == me
+    event = lax.broadcasted_iota(jnp.int32, (extra, ntok), 1) == off_ref[0]
+    pick = jnp.where(spot & event, 1.0, 0.0).astype(jnp.bfloat16)
+    tok[z, pl.ds(ntok, extra), :] = jnp.dot(
+        pick, tok[z, pl.ds(0, ntok), :], preferred_element_type=jnp.float32
+    ).astype(jnp.bfloat16)
+
+    def tok_up(source):
+        return remote(tok.at[source], tok.at[source], t_send.at[0, source], t_recv.at[source], at(z + 1, lane))
+
+    def tok_down(source):
+        return remote(tok.at[source], tok.at[source], t_send.at[1, source], t_recv.at[source], at(z - 1, lane))
+
+    can_up, can_down = z + 1 < planes, z >= 1
+
+    @pl.when(can_up)
+    def _():
+        tok_up(z).start()
+
+    @pl.when(can_down)
+    def _():
+        tok_down(z).start()
+
+    def pass_on(dist):
+        @pl.when(z >= dist)
+        def _():
+            tok_up_or_recv(z - dist)
+
+            @pl.when(can_up)
+            def _():
+                tok_up(z - dist).start()
+
+        @pl.when(z + dist < planes)
+        def _():
+            tok_up_or_recv(z + dist)
+
+            @pl.when(can_down)
+            def _():
+                tok_down(z + dist).start()
+
+    def tok_up_or_recv(source):
+        remote(tok.at[source], tok.at[source], t_send.at[0, source], t_recv.at[source], core_peer).wait_recv()
+
+    for copy in own_w:
+        copy.wait()
+    for step in range(1, planes):
+        for part in range(3):
+            weight_landed(step, part).wait_recv()
+    x_out = remote(wts.at[:, lane, x], wts.at[:, lane, x], wx_send, wx_recv, x_peer)
+    x_out.start()
+    x_in = remote(wts.at[:, lane, 1 - x], wts.at[:, lane, 1 - x], wx_send, wx_recv, x_peer)
+    x_in.wait_recv()
+
+    def lane_copy(which, index, peer):
+        return remote(wts.at[:, which], wts.at[:, which], wl_send.at[index], wl_recv.at[index], peer)
+
+    lane_copy(lane, 0, y_peer).start()
+    lane_copy(lane, 1, core_peer).start()
+    if planes > 1:
+        pass_on(1)
+    lane_copy(y_lane, 0, y_peer).wait_recv()
+    lane_copy(y_lane, 2, core_peer).start()
+    lane_copy(core_lane, 1, core_peer).wait_recv()
+    lane_copy(diag_lane, 2, core_peer).wait_recv()
+
+    def order_of(plane):
+        return sorted(range(planes), key=lambda p: (abs(p - plane), p))
+
+    def nth(index):
+        value = jnp.int32(order_of(0)[index])
+        for plane in range(1, planes):
+            value = jnp.where(z == plane, order_of(plane)[index], value)
+        return value
+
+    order = [nth(i) for i in range(planes)]
+
+    def kv_rows(plane, where):
+        return kv.at[pl.ds((plane * LANES + where) * nblk, nblk)]
+
+    def kv_copy(index, which, where, peer):
+        ref = kv_rows(order[index], where)
+        return remote(ref, ref, k_send.at[which, index], k_recv.at[which, index], peer)
+
+    def project(index):
+        p = order[index]
+        weights = wts[...].reshape(-1, 3 * cols)
+        res = jnp.dot(tok[p], weights, preferred_element_type=jnp.float32)
+        res = res.astype(jnp.bfloat16)
+        qry[p] = res[:ntok, :cols]
+        kv_rows(p, lane)[...] = res[:ntok, cols:].reshape(nblk, BLOCK, 2 * cols)
+        events[lane, p] = res[ntok:, cols:]
+        kv_copy(index, 0, lane, y_peer).start()
+        kv_copy(index, 1, lane, core_peer).start()
+
+    def kv_forward(index):
+        kv_copy(index, 0, y_lane, y_peer).wait_recv()
+        kv_copy(index, 2, y_lane, core_peer).start()
+
+    project(0)
+    for index in range(1, planes):
+        if index > 1:
+            pass_on(index)
+        project(index)
+        kv_forward(index - 1)
+
+    def event_copy(index, where, peer):
+        return remote(events.at[where], events.at[where], e_send.at[index], e_recv.at[index], peer)
+
+    partners = ((y_lane, y_peer), (core_lane, core_peer), (diag_lane, diag_peer))
+    for index, (where, peer) in enumerate(partners):
+        event_copy(index, lane, peer).start()
+    kv_forward(planes - 1)
+    for index in range(planes):
+        kv_copy(index, 1, core_lane, core_peer).wait_recv()
+        kv_copy(index, 2, diag_lane, core_peer).wait_recv()
+
+    for index, (where, peer) in enumerate(partners):
+        event_copy(index, where, peer).wait_recv()
+    glob = events[...].reshape(LANES * planes, extra, 2 * cols).astype(jnp.float32)
+    glob = jnp.sum(glob, axis=0)[: planes * LANES].astype(jnp.bfloat16)
+    total_blocks = planes * LANES * nblk
+    scale = HD ** (-0.5)
+    keys = (3 + R) * BLOCK + glob.shape[0]
+    column = lax.broadcasted_iota(jnp.int32, (BLOCK, keys), 1)
+
+    def ctx_copy(plane, index):
+        return remote(
+            ctx.at[plane],
+            out_ref.at[:, pl.ds(pl.multiple_of(z * cols, cols), cols)],
+            c_send.at[index], c_recv.at[z], at(plane, lane),
+        )
+
+    def attend(plane):
+        def body(sub, carry):
+            block = (plane * LANES + lane) * nblk + sub
+            starts = [
+                jnp.maximum(block - 1, 0),
+                block,
+                jnp.minimum(block + 1, total_blocks - 1),
+            ]
+            hidden = ((column < BLOCK) & (block == 0)) | (
+                (column >= 2 * BLOCK) & (column < 3 * BLOCK) & (block == total_blocks - 1)
+            )
+            q_rows = pl.ds(pl.multiple_of(sub * BLOCK, BLOCK), BLOCK)
+            for h in range(heads):
+                base = (block * H + z * heads + h) * R
+                where = starts + [blocks_ref[base + j] for j in range(R)]
+                k_cols = slice(h * HD, (h + 1) * HD)
+                v_cols = slice(cols + h * HD, cols + (h + 1) * HD)
+                key = jnp.concatenate(
+                    [kv[w, :, k_cols] for w in where] + [glob[:, k_cols]], axis=0
+                )
+                val = jnp.concatenate(
+                    [kv[w, :, v_cols] for w in where] + [glob[:, v_cols]], axis=0
+                )
+                score = lax.dot_general(
+                    qry[plane, q_rows, k_cols], key, (((1,), (1,)), ((), ())),
+                    preferred_element_type=jnp.float32,
+                ) * scale
+                score = jnp.where(hidden, -jnp.inf, score)
+                expo = jnp.exp(score - jnp.max(score, axis=1, keepdims=True))
+                soft = (expo / jnp.sum(expo, axis=1, keepdims=True)).astype(jnp.bfloat16)
+                ctx[plane, q_rows, k_cols] = jnp.dot(
+                    soft, val, preferred_element_type=jnp.float32
+                ).astype(jnp.bfloat16)
+            return carry
+
+        lax.fori_loop(0, nblk, body, 0)
+
+    for index in range(planes - 1, 0, -1):
+        attend(order[index])
+        ctx_copy(order[index], index).start()
+    attend(z)
+    own = pltpu.make_async_copy(
+        ctx.at[z], out_ref.at[:, pl.ds(pl.multiple_of(z * cols, cols), cols)], local_sem.at[0]
+    )
+    own.start()
+    own.wait()
+
+    for index in range(1, planes):
+        ctx_copy(order[index], index).wait_send()
+        plane = order[index]
+        there = out_ref.at[:, pl.ds(pl.multiple_of(plane * cols, cols), cols)]
+        remote(ctx.at[plane], there, c_send.at[index], c_recv.at[plane], core_peer).wait_recv()
+    for step in range(1, planes):
+        for part in range(3):
+            weight_copy(step, part).wait_send()
+    x_out.wait_send()
+    lane_copy(lane, 0, y_peer).wait_send()
+    lane_copy(lane, 1, core_peer).wait_send()
+    lane_copy(y_lane, 2, core_peer).wait_send()
+    for index in range(planes):
+        kv_copy(index, 0, lane, y_peer).wait_send()
+        kv_copy(index, 1, lane, core_peer).wait_send()
+        kv_copy(index, 2, y_lane, core_peer).wait_send()
+    for index, (where, peer) in enumerate(partners):
+        event_copy(index, lane, peer).wait_send()
+    for source in range(planes):
+        @pl.when(can_up & (z >= source))
+        def _():
+            tok_up(source).wait_send()
+
+        @pl.when(can_down & (z <= source))
+        def _():
+            tok_down(source).wait_send()
+
+
+def fused(tokens, w_query, w_keyval, global_off, rand_dev, rand_sub):
+    nseq = lax.axis_size("seq")
+    ntok, width = tokens.shape
+    planes = nseq // LANES
+    extra = -(-nseq // 16) * 16
+    slot_rows = ntok + extra
+    cols = H // planes * HD
+    half = w_query.shape[0] // 2
+    rows = (rand_dev * (ntok // BLOCK) + rand_sub).reshape(-1)
+    dma = pltpu.SemaphoreType.DMA
+    steps = max(planes - 1, 1)
+    return pl.pallas_call(
+        functools.partial(fused_kernel, planes),
+        out_shape=jax.ShapeDtypeStruct((ntok, H * HD), jnp.bfloat16),
+        in_specs=[pl.BlockSpec(memory_space=pl.ANY)] * 3
+        + [pl.BlockSpec(memory_space=pltpu.SMEM)] * 2,
+        out_specs=pl.BlockSpec(memory_space=pl.ANY),
+        scratch_shapes=[
+            pltpu.VMEM((planes, slot_rows, width), jnp.bfloat16),
+            pltpu.VMEM((planes, LANES, 2, half, 3 * cols), jnp.bfloat16),
+            pltpu.VMEM((planes, ntok, cols), jnp.bfloat16),
+            pltpu.VMEM((nseq * ntok // BLOCK, BLOCK, 2 * cols), jnp.bfloat16),
+            pltpu.VMEM((LANES, planes, extra, 2 * cols), jnp.bfloat16),
+            pltpu.VMEM((planes, ntok, cols), jnp.bfloat16),
+            dma((4,)),
+            dma((steps, 3)),
+            dma((steps, 3)),
+            dma,
+            dma,
+            dma((3,)),
+            dma((3,)),
+            dma((2, planes)),
+            dma((planes,)),
+            dma((3, planes)),
+            dma((3, planes)),
+            dma((3,)),
+            dma((3,)),
+            dma((planes,)),
+            dma((planes,)),
+        ],
+        compiler_params=pltpu.CompilerParams(
+            collective_id=0, has_side_effects=True, vmem_limit_bytes=48 * 1024 * 1024
+        ),
+        cost_estimate=pl.CostEstimate(
+            flops=2 * planes * slot_rows * width * 3 * cols,
+            bytes_accessed=2 * planes * slot_rows * width,
+            transcendentals=ntok * H * 400,
+        ),
+    )(tokens, w_query, w_keyval, global_off, rows)
+
+
 def solution(mesh):
     in_specs = (
         P(("groups", "seq"), None),
@@ -120,4 +466,8 @@
         P("groups", None, None),
     )
     out_specs = P(("groups", "seq"), None)
-    return jax.shard_map(local, mesh=mesh, in_specs=in_specs, out_specs=out_specs, check_vma=False)
+    nseq, groups = mesh.shape["seq"], mesh.shape["groups"]
+    planes = nseq // LANES
+    whole_heads = groups == 2 and planes * LANES == nseq and H % planes == 0
+    body = fused if whole_heads else local
+    return jax.shard_map(body, mesh=mesh, in_specs=in_specs, out_specs=out_specs, check_vma=False)

time: 280 us -> 120 us (0.43)
  the two profiles are of different devices: /device:TPU:13 before, /device:TPU:0 now
where the time goes in v1:
time: 120 us; the launch traced here: 118 us
  Pallas kernels  113 us (94%)
  local copies, waits for them, and re-layouts  3.35 us (3%)
    pallas_call x1, Pallas kernels, fused(): pl.pallas_call(functools.partial(fused_kernel, planes), out_shape=jax.Sha...  113 us
    unnamed x7, local copies, waits for them, and re-layouts  2.97 us

profile of v1, /device:TPU:0, one launch (start us, length us, event | category | flops | bytes accessed | tf_op | source)
XLA Modules:
  0.0 117.5 jit_solution(1279794016393570782)
XLA Ops:
  0.0 0.0 copy-start.1
  0.7 0.7 multiply_add_fusion
  1.4 0.2 copy.7
  1.6 0.2 reshape.3.blocks_ref
  1.8 0.0 copy-done.1
  1.8 0.0 copy-start
  1.9 1.2 %copy-done = bf16[256,2048]{1,0:T(8,128)(2,1)S(1)} copy-done((bf16[256,2048]{1,0:T(8,128)(2,1)S(1)}, bf16[256,2048]{1,0:T(8,128)(2,1)}, u32[]{:S(2)}) %copy-start) | copy-done | bytes 1048600
  3.1 0.0 copy-start.2
  3.1 0.9 copy-done.2
  4.0 112.7 %shard_map.64 = bf16[256,1024]{1,0:T(8,128)(2,1)S(1)} custom-call(bf16[256,2048]{1,0:T(8,128)(2,1)S(1)} %copy-done, bf16[128,1024]{1,0:T(8,128)(2,1)S(1)} %copy-done.2, bf16[128,2048]{1,0:T(8,128)(2,1)S(1)} %copy-done.1, s32[1]{0:T(128)S(6)} %copy.9.off_ref, s32[1536]{0:T(1024)S(1)} %reshape.3.blocks_ref), custom_call_target="tpu_custom_call" | custom-call | flops 3422552064 | bytes 4456448 | tf_op jit(solution)/shard_map/pallas_call | solution.py:419
  116.7 0.8 copy.10
Async XLA Ops:
  0.0 1.8 %copy-start.1 = (bf16[128,2048]{1,0:T(8,128)(2,1)S(1)}, bf16[128,2048]{1,0:T(8,128)(2,1)}, u32[]{:S(2)}) copy-start(bf16[128,2048]{1,0:T(8,128)(2,1)} %wkv_hbm.1) | copy-start | bytes 1572868
  1.8 1.2 %copy-start = (bf16[256,2048]{1,0:T(8,128)(2,1)S(1)}, bf16[256,2048]{1,0:T(8,128)(2,1)}, u32[]{:S(2)}) copy-start(bf16[256,2048]{1,0:T(8,128)(2,1)} %tok_hbm.1) | copy-start | bytes 3145732
  3.1 0.9 copy-start.2

commit v2 on v0

--- a/solution.py
+++ b/solution.py
@@ -1,6 +1,10 @@
+import functools
+
 import jax
 import jax.numpy as jnp
 from jax import lax
+from jax.experimental import pallas as pl
+from jax.experimental.pallas import tpu as pltpu
 from jax.sharding import PartitionSpec as P
 
 H = 8
@@ -8,6 +12,8 @@
 BLOCK = 64
 R = 3
 BLK_DEV = 4
+LANES = 4
+MESH = pl.DeviceIdType.MESH
 
 
 def padded_2(block, sides, width):
@@ -110,6 +116,413 @@
     return ctx.reshape(ntok, inner).astype(jnp.bfloat16)
 
 
+def fused_kernel(
+    planes, tok_hbm, wq_hbm, wkv_hbm, pick_hbm, blocks_hbm, out_ref,
+    tok, wts, qry, kv, far_q, far_kv, picks, ctx, blocks_ref,
+    local_sem, w_send, w_recv, g_send, g_recv, t_send, t_recv, f_send, f_recv,
+    k_send, k_recv, p_send, p_recv, o_send, o_recv, c_send, c_recv,
+):
+    ntok = tok_hbm.shape[0]
+    nblk = ntok // BLOCK
+    heads = H // planes
+    cols = heads * HD
+    half = wts.shape[4]
+    x = lax.axis_index("groups")
+    me = lax.axis_index("seq")
+    z = me // LANES
+    lane = me % LANES
+    core_lane = lane + 1 - 2 * (lane % 2)
+    y_lane = (lane + 2) % LANES
+    diag_lane = (core_lane + 2) % LANES
+    mid = planes // 2
+    workers, ends = (mid - 1, mid), (0, planes - 1)
+    lower = z < mid
+    own_worker = jnp.where(lower, workers[0], workers[1])
+    own_end = jnp.where(lower, ends[0], ends[1])
+    far_worker = jnp.where(lower, workers[1], workers[0])
+    far_end = jnp.where(lower, ends[1], ends[0])
+    mate = jnp.where(z == own_worker, own_end, own_worker)
+    order = [own_worker, own_end, far_worker, far_end]
+
+    def at(plane, where):
+        return {"seq": plane * LANES + where}
+
+    x_peer = {"groups": 1 - x}
+    core_peer = at(z, core_lane)
+    y_peer = at(z, y_lane)
+    diag_peer = at(z, diag_lane)
+    partners = ((y_lane, y_peer), (core_lane, core_peer), (diag_lane, diag_peer))
+
+    def remote(src, dst, send, recv, peer):
+        return pltpu.make_async_remote_copy(
+            src_ref=src, dst_ref=dst, send_sem=send, recv_sem=recv, device_id=peer,
+            device_id_type=MESH,
+        )
+
+    blocks_in = pltpu.make_async_copy(blocks_hbm, blocks_ref, local_sem.at[0])
+    blocks_in.start()
+    pick_in = pltpu.make_async_copy(pick_hbm, picks.at[lane, z], local_sem.at[1])
+    pick_in.start()
+    tok_in = pltpu.make_async_copy(tok_hbm, tok.at[z], local_sem.at[2])
+    tok_in.start()
+
+    barrier = pltpu.get_barrier_semaphore()
+    for step in range(1, planes):
+        pl.semaphore_signal(
+            barrier, inc=1, device_id=at((z + step) % planes, lane), device_id_type=MESH
+        )
+    for peer in (x_peer, core_peer, y_peer, diag_peer):
+        pl.semaphore_signal(barrier, inc=1, device_id=peer, device_id_type=MESH)
+    pl.semaphore_wait(barrier, planes - 1 + 4)
+
+    def weight_refs(index, kind, part):
+        plane = (ends, workers)[kind][index]
+        rows = pl.ds(pl.multiple_of(x * half, half), half)
+        first = (0, 0, H * HD)[part] + plane * cols
+        src = (wq_hbm, wkv_hbm, wkv_hbm)[part].at[rows, pl.ds(first, cols)]
+        return src, wts.at[kind, z, lane, x, :, pl.ds(part * cols, cols)]
+
+    def weight_remote(index, kind, part):
+        src, dst = weight_refs(index, kind, part)
+        return remote(
+            src, dst, w_send.at[index, kind, part], w_recv.at[z, kind, part],
+            at(workers[index], lane),
+        )
+
+    def weights_out(kind):
+        for index in range(2):
+            for part in range(3):
+                @pl.when(z != workers[index])
+                def _():
+                    weight_remote(index, kind, part).start()
+
+                @pl.when(z == workers[index])
+                def _():
+                    src, dst = weight_refs(index, kind, part)
+                    pltpu.make_async_copy(src, dst, w_recv.at[z, kind, part]).start()
+
+    def weights_in(kind):
+        for plane in range(planes):
+            for part in range(3):
+                here = wts.at[kind, plane, lane, x, :, pl.ds(part * cols, cols)]
+                remote(here, here, w_send.at[0, kind, part], w_recv.at[plane, kind, part], core_peer).wait_recv()
+
+    towards = jnp.where(lower, z + 1, z - 1)
+    own_out = remote(tok_hbm, tok.at[z], t_send.at[0], t_recv.at[z], at(towards, lane))
+    pass_out = remote(
+        tok.at[own_end], tok.at[own_end], t_send.at[1], t_recv.at[own_end], at(towards, lane)
+    )
+
+    def tok_wait(plane):
+        remote(tok.at[plane], tok.at[plane], t_send.at[0], t_recv.at[plane], core_peer).wait_recv()
+
+    weights_out(0)
+    own_out.start()
+    weights_out(1)
+    pick_in.wait()
+
+    def pick_copy(step):
+        ref = picks.at[lane, z]
+        return remote(ref, ref, p_send.at[step - 1], p_recv.at[z], at((z + step) % planes, lane))
+
+    for step in range(1, planes):
+        pick_copy(step).start()
+
+    width = 3 * cols
+    every, left, right = pl.ds(0, width), pl.ds(0, width // 2), pl.ds(width // 2, width // 2)
+    moves = (
+        (x, lane, every, x_peer, 1 - x, lane),
+        (x, lane, every, y_peer, x, y_lane),
+        (x, lane, every, core_peer, x, core_lane),
+        (1 - x, lane, left, y_peer, 1 - x, y_lane),
+        (1 - x, lane, every, core_peer, 1 - x, core_lane),
+        (x, y_lane, right, x_peer, 1 - x, y_lane),
+        (x, y_lane, every, core_peer, x, diag_lane),
+        (1 - x, y_lane, left, core_peer, 1 - x, diag_lane),
+        (1 - x, y_lane, right, core_peer, 1 - x, diag_lane),
+    )
+
+    def gather_out(kind, index):
+        group, where, part, peer = moves[index][:4]
+        ref = wts.at[kind, :, where, group, :, part]
+        return remote(ref, ref, g_send.at[kind, index], g_recv.at[kind, index], peer)
+
+    def gather_wait(kind, index):
+        part, peer, group, where = moves[index][2:]
+        ref = wts.at[kind, :, where, group, :, part]
+        remote(ref, ref, g_send.at[kind, index], g_recv.at[kind, index], peer).wait_recv()
+
+    def gather_first(kind):
+        weights_in(kind)
+        for index in range(3):
+            gather_out(kind, index).start()
+
+    def gather_second(kind):
+        gather_wait(kind, 0)
+        gather_out(kind, 3).start()
+        gather_out(kind, 4).start()
+        gather_wait(kind, 1)
+        gather_out(kind, 5).start()
+        gather_out(kind, 6).start()
+
+    def gather_last(kind):
+        gather_wait(kind, 3)
+        gather_out(kind, 7).start()
+        gather_wait(kind, 5)
+        gather_out(kind, 8).start()
+        for index in (2, 4, 6, 7, 8):
+            gather_wait(kind, index)
+
+    def kv_rows(ref, plane, where):
+        return ref.at[pl.ds((plane * LANES + where) * nblk, nblk)]
+
+    def kv_copy(index, which, where, peer):
+        ref = kv_rows(kv, order[index], where)
+        return remote(ref, ref, k_send.at[which, index], k_recv.at[which, index], peer)
+
+    def kv_out(index):
+        kv_copy(index, 0, lane, y_peer).start()
+        kv_copy(index, 1, lane, core_peer).start()
+
+    def kv_forward(index):
+        kv_copy(index, 0, y_lane, y_peer).wait_recv()
+        kv_copy(index, 2, y_lane, core_peer).start()
+
+    def project(index, kind):
+        weights = wts[kind].reshape(-1, width)
+        res = jnp.dot(tok[order[index]], weights, preferred_element_type=jnp.float32)
+        return res.astype(jnp.bfloat16)
+
+    def far_copies(index):
+        p = order[index]
+        return (
+            remote(far_q.at[index], qry.at[p], f_send.at[0, index], f_recv.at[0, index], at(mate, lane)),
+            remote(
+                far_kv.at[index], kv_rows(kv, p, lane), f_send.at[1, index], f_recv.at[1, index],
+                at(mate, lane),
+            ),
+        )
+
+    def project_far(index):
+        res = project(index, 0)
+        far_q[index] = res[:, :cols]
+        far_kv[index] = res[:, cols:].reshape(nblk, BLOCK, 2 * cols)
+        for copy in far_copies(index):
+            copy.start()
+
+    def project_own(index):
+        res = project(index, 1)
+        qry[order[index]] = res[:, :cols]
+        kv_rows(kv, order[index], lane)[...] = res[:, cols:].reshape(nblk, BLOCK, 2 * cols)
+        kv_out(index)
+
+    @pl.when(z == own_worker)
+    def _():
+        gather_first(0)
+        tok_in.wait()
+        tok_wait(own_end)
+        pass_out.start()
+        gather_second(0)
+        gather_first(1)
+        gather_last(0)
+        project_far(0)
+        project_far(1)
+        gather_second(1)
+        tok_wait(far_worker)
+        project_far(2)
+        gather_last(1)
+        project_own(0)
+        project_own(1)
+        kv_forward(0)
+        project_own(2)
+        kv_forward(1)
+        tok_wait(far_end)
+        project_far(3)
+        project_own(3)
+        kv_forward(2)
+        kv_forward(3)
+
+    @pl.when(z != own_worker)
+    def _():
+        tok_in.wait()
+        for index in range(planes):
+            here_q, here_kv = qry.at[order[index]], kv_rows(kv, order[index], lane)
+            remote(here_kv, here_kv, f_send.at[1, index], f_recv.at[1, index], core_peer).wait_recv()
+            kv_out(index)
+            remote(here_q, here_q, f_send.at[0, index], f_recv.at[0, index], core_peer).wait_recv()
+            if index:
+                kv_forward(index - 1)
+        kv_forward(planes - 1)
+
+    for step in range(1, planes):
+        source = (z + step) % planes
+        ref = picks.at[lane, source]
+        remote(ref, ref, p_send.at[0], p_recv.at[source], core_peer).wait_recv()
+
+    def pick_lane(index, where, peer):
+        return remote(picks.at[where], picks.at[where], o_send.at[index], o_recv.at[index], peer)
+
+    for index, (where, peer) in enumerate(partners):
+        pick_lane(index, lane, peer).start()
+    for index, (where, peer) in enumerate(partners):
+        pick_lane(index, where, peer).wait_recv()
+    glob = jnp.zeros((picks.shape[2], 2 * cols), jnp.float32)
+    for index in range(planes):
+        kv_copy(index, 1, core_lane, core_peer).wait_recv()
+        kv_copy(index, 2, diag_lane, core_peer).wait_recv()
+    for plane in range(planes):
+        for where in range(LANES):
+            rows = kv_rows(kv, plane, where)[...].reshape(ntok, 2 * cols)
+            glob = glob + jnp.dot(picks[where, plane], rows, preferred_element_type=jnp.float32)
+    glob = glob[: planes * LANES].astype(jnp.bfloat16)
+    blocks_in.wait()
+    total_blocks = planes * LANES * nblk
+    scale = HD ** (-0.5)
+    keys = (3 + R) * BLOCK + glob.shape[0]
+    column = lax.broadcasted_iota(jnp.int32, (BLOCK, keys), 1)
+
+    def ctx_copy(plane, index):
+        return remote(
+            ctx.at[plane],
+            out_ref.at[:, pl.ds(pl.multiple_of(z * cols, cols), cols)],
+            c_send.at[index], c_recv.at[z], at(plane, lane),
+        )
+
+    def attend(plane):
+        for sub in range(nblk):
+            block = (plane * LANES + lane) * nblk + sub
+            starts = [
+                jnp.maximum(block - 1, 0),
+                block,
+                jnp.minimum(block + 1, total_blocks - 1),
+            ]
+            hidden = ((column < BLOCK) & (block == 0)) | (
+                (column >= 2 * BLOCK) & (column < 3 * BLOCK) & (block == total_blocks - 1)
+            )
+            q_rows = slice(sub * BLOCK, (sub + 1) * BLOCK)
+            for h in range(heads):
+                base = (block * H + z * heads + h) * R
+                where = starts + [blocks_ref[base + j] for j in range(R)]
+                k_cols = slice(h * HD, (h + 1) * HD)
+                v_cols = slice(cols + h * HD, cols + (h + 1) * HD)
+                key = jnp.concatenate(
+                    [kv[w, :, k_cols] for w in where] + [glob[:, k_cols]], axis=0
+                )
+                val = jnp.concatenate(
+                    [kv[w, :, v_cols] for w in where] + [glob[:, v_cols]], axis=0
+                )
+                score = lax.dot_general(
+                    qry[plane, q_rows, k_cols], key, (((1,), (1,)), ((), ())),
+                    preferred_element_type=jnp.float32,
+                ) * scale
+                score = jnp.where(hidden, -jnp.inf, score)
+                expo = jnp.exp(score - jnp.max(score, axis=1, keepdims=True))
+                soft = (expo / jnp.sum(expo, axis=1, keepdims=True)).astype(jnp.bfloat16)
+                ctx[plane, q_rows, k_cols] = jnp.dot(
+                    soft, val, preferred_element_type=jnp.float32
+                ).astype(jnp.bfloat16)
+
+    others = (far_end, far_worker, mate)
+    for index, plane in enumerate(others):
+        attend(plane)
+        ctx_copy(plane, index).start()
+    attend(z)
+    own = pltpu.make_async_copy(
+        ctx.at[z], out_ref.at[:, pl.ds(pl.multiple_of(z * cols, cols), cols)], local_sem.at[0]
+    )
+    own.start()
+    own.wait()
+
+    for index, plane in enumerate(others):
+        ctx_copy(plane, index).wait_send()
+        there = out_ref.at[:, pl.ds(pl.multiple_of(plane * cols, cols), cols)]
+        remote(ctx.at[plane], there, c_send.at[index], c_recv.at[plane], core_peer).wait_recv()
+    for index in range(2):
+        @pl.when(z != workers[index])
+        def _():
+            for kind in range(2):
+                for part in range(3):
+                    weight_remote(index, kind, part).wait_send()
+    own_out.wait_send()
+
+    @pl.when(z == own_worker)
+    def _():
+        pass_out.wait_send()
+        for kind in range(2):
+            for index in range(len(moves)):
+                gather_out(kind, index).wait_send()
+        for index in range(planes):
+            for copy in far_copies(index):
+                copy.wait_send()
+
+    for index in range(planes):
+        kv_copy(index, 0, lane, y_peer).wait_send()
+        kv_copy(index, 1, lane, core_peer).wait_send()
+        kv_copy(index, 2, y_lane, core_peer).wait_send()
+    for step in range(1, planes):
+        pick_copy(step).wait_send()
+    for index, (where, peer) in enumerate(partners):
+        pick_lane(index, lane, peer).wait_send()
+
+
+def fused(tokens, w_query, w_keyval, global_off, rand_dev, rand_sub):
+    nseq = lax.axis_size("seq")
+    ntok, width = tokens.shape
+    planes = nseq // LANES
+    nblk = ntok // BLOCK
+    picked = -(-nseq // 16) * 16
+    cols = H // planes * HD
+    half = w_query.shape[0] // 2
+    blocks = (rand_dev * nblk + rand_sub).reshape(-1)
+    shape = (picked, ntok)
+    at_row = lax.broadcasted_iota(jnp.int32, shape, 0) == lax.axis_index("seq")
+    at_event = lax.broadcasted_iota(jnp.int32, shape, 1) == global_off[0]
+    pick = jnp.where(at_row & at_event, 1.0, 0.0).astype(jnp.bfloat16)
+    dma = pltpu.SemaphoreType.DMA
+    return pl.pallas_call(
+        functools.partial(fused_kernel, planes),
+        out_shape=jax.ShapeDtypeStruct((ntok, H * HD), jnp.bfloat16),
+        in_specs=[pl.BlockSpec(memory_space=pl.ANY)] * 5,
+        out_specs=pl.BlockSpec(memory_space=pl.ANY),
+        scratch_shapes=[
+            pltpu.VMEM((planes, ntok, width), jnp.bfloat16),
+            pltpu.VMEM((2, planes, LANES, 2, half, 3 * cols), jnp.bfloat16),
+            pltpu.VMEM((planes, ntok, cols), jnp.bfloat16),
+            pltpu.VMEM((nseq * nblk, BLOCK, 2 * cols), jnp.bfloat16),
+            pltpu.VMEM((planes, ntok, cols), jnp.bfloat16),
+            pltpu.VMEM((planes, nblk, BLOCK, 2 * cols), jnp.bfloat16),
+            pltpu.VMEM((LANES, planes, picked, ntok), jnp.bfloat16),
+            pltpu.VMEM((planes, ntok, cols), jnp.bfloat16),
+            pltpu.SMEM(blocks.shape, jnp.int32),
+            dma((3,)),
+            dma((2, 2, 3)),
+            dma((planes, 2, 3)),
+            dma((2, 9)),
+            dma((2, 9)),
+            dma((2,)),
+            dma((planes,)),
+            dma((2, planes)),
+            dma((2, planes)),
+            dma((3, planes)),
+            dma((3, planes)),
+            dma((planes - 1,)),
+            dma((planes,)),
+            dma((3,)),
+            dma((3,)),
+            dma((planes - 1,)),
+            dma((planes,)),
+        ],
+        compiler_params=pltpu.CompilerParams(
+            collective_id=0, has_side_effects=True, vmem_limit_bytes=48 * 1024 * 1024
+        ),
+        cost_estimate=pl.CostEstimate(
+            flops=2 * planes * ntok * width * 3 * cols,
+            bytes_accessed=2 * planes * ntok * width,
+            transcendentals=ntok * H * 400,
+        ),
+    )(tokens, w_query, w_keyval, pick, blocks)
+
+
 def solution(mesh):
     in_specs = (
         P(("groups", "seq"), None),
@@ -120,4 +533,8 @@
         P("groups", None, None),
     )
     out_specs = P(("groups", "seq"), None)
-    return jax.shard_map(local, mesh=mesh, in_specs=in_specs, out_specs=out_specs, check_vma=False)
+    nseq, groups = mesh.shape["seq"], mesh.shape["groups"]
+    planes = nseq // LANES
+    paired = groups == 2 and planes * LANES == nseq and planes == 4
+    body = fused if paired else local
+    return jax.shard_map(body, mesh=mesh, in_specs=in_specs, out_specs=out_specs, check_vma=False)

time: 280 us -> 110 us (0.39)
  the two profiles are of different devices: /device:TPU:13 before, /device:TPU:0 now
where the time goes in v2:
time: 110 us; the launch traced here: 108 us
  Pallas kernels  103 us (94%)
  local copies, waits for them, and re-layouts  3.35 us (3%)
    pallas_call x1, Pallas kernels, fused(): pl.pallas_call(functools.partial(fused_kernel, planes), out_shape=jax.Sha...  103 us
    unnamed x9, local copies, waits for them, and re-layouts  2.97 us

profile of v2, /device:TPU:0, one launch (start us, length us, event | category | flops | bytes accessed | tf_op | source)
XLA Modules:
  0.0 108.4 jit_solution(6408294585333590463)
XLA Ops:
  0.0 0.0 copy-start.3
  0.0 0.0 copy-start.1
  0.7 0.1 select_convert_fusion.pick_hbm
  0.8 0.0 copy-done.3
  0.8 0.7 multiply_add_fusion
  1.5 0.2 copy.7
  1.7 0.2 reshape.3.blocks_hbm
  1.9 0.0 copy-done.1
  1.9 0.0 copy-start
  1.9 1.2 %copy-done = bf16[256,2048]{1,0:T(8,128)(2,1)S(1)} copy-done((bf16[256,2048]{1,0:T(8,128)(2,1)S(1)}, bf16[256,2048]{1,0:T(8,128)(2,1)}, u32[]{:S(2)}) %copy-start) | copy-done | bytes 1048600
  3.2 0.0 copy-start.2
  3.2 0.9 copy-done.2
  4.1 103.5 %shard_map.64 = bf16[256,1024]{1,0:T(8,128)(2,1)S(1)} custom-call(bf16[256,2048]{1,0:T(8,128)(2,1)S(1)} %copy-done, bf16[128,1024]{1,0:T(8,128)(2,1)S(1)} %copy-done.2, bf16[128,2048]{1,0:T(8,128)(2,1)S(1)} %copy-done.1, bf16[16,256]{1,0:T(8,128)(2,1)S(1)} %select_convert_fusion.pick_hbm, s32[1536]{0:T(1024)S(1)} %reshape.3.blocks_hbm), custom_call_target="tpu_custom_call" | custom-call | flops 3221225472 | bytes 4194304 | tf_op jit(solution)/shard_map/pallas_call | solution.py:482
  107.6 0.8 copy.10
  (2 shorter events, 0.0 us)
Async XLA Ops:
  0.0 0.8 copy-start.3
  0.0 1.9 %copy-start.1 = (bf16[128,2048]{1,0:T(8,128)(2,1)S(1)}, bf16[128,2048]{1,0:T(8,128)(2,1)}, u32[]{:S(2)}) copy-start(bf16[128,2048]{1,0:T(8,128)(2,1)} %wkv_hbm.1) | copy-start | bytes 1572868
  1.9 1.2 %copy-start = (bf16[256,2048]{1,0:T(8,128)(2,1)S(1)}, bf16[256,2048]{1,0:T(8,128)(2,1)}, u32[]{:S(2)}) copy-start(bf16[256,2048]{1,0:T(8,128)(2,1)} %tok_hbm.1) | copy-start | bytes 3145732
  3.2 0.9 copy-start.2

commit v3 on v2

--- a/solution.py
+++ b/solution.py
@@ -117,8 +117,8 @@
 
 
 def fused_kernel(
-    planes, tok_hbm, wq_hbm, wkv_hbm, pick_hbm, blocks_hbm, out_ref,
-    tok, wts, qry, kv, far_q, far_kv, picks, ctx, blocks_ref,
+    planes, tok_hbm, wq_hbm, wkv_hbm, pick_hbm, dev_hbm, sub_hbm, out_ref,
+    tok, wts, qry, kv, far_q, far_kv, picks, ctx, dev_ref, sub_ref,
     local_sem, w_send, w_recv, g_send, g_recv, t_send, t_recv, f_send, f_recv,
     k_send, k_recv, p_send, p_recv, o_send, o_recv, c_send, c_recv,
 ):
@@ -159,8 +159,10 @@
             device_id_type=MESH,
         )
 
-    blocks_in = pltpu.make_async_copy(blocks_hbm, blocks_ref, local_sem.at[0])
-    blocks_in.start()
+    dev_in = pltpu.make_async_copy(dev_hbm, dev_ref, local_sem.at[0])
+    dev_in.start()
+    sub_in = pltpu.make_async_copy(sub_hbm, sub_ref, local_sem.at[3])
+    sub_in.start()
     pick_in = pltpu.make_async_copy(pick_hbm, picks.at[lane, z], local_sem.at[1])
     pick_in.start()
     tok_in = pltpu.make_async_copy(tok_hbm, tok.at[z], local_sem.at[2])
@@ -208,17 +210,27 @@
                 remote(here, here, w_send.at[0, kind, part], w_recv.at[plane, kind, part], core_peer).wait_recv()
 
     towards = jnp.where(lower, z + 1, z - 1)
-    own_out = remote(tok_hbm, tok.at[z], t_send.at[0], t_recv.at[z], at(towards, lane))
-    pass_out = remote(
-        tok.at[own_end], tok.at[own_end], t_send.at[1], t_recv.at[own_end], at(towards, lane)
-    )
-
-    def tok_wait(plane):
-        remote(tok.at[plane], tok.at[plane], t_send.at[0], t_recv.at[plane], core_peer).wait_recv()
+    chunk = ntok // 2
+    chunks = (pl.ds(0, chunk), pl.ds(chunk, chunk))
+
+    def own_out(c):
+        return remote(
+            tok_hbm.at[chunks[c]], tok.at[z, chunks[c]], t_send.at[0, c], t_recv.at[z, c],
+            at(towards, lane),
+        )
+
+    def pass_out(c):
+        ref = tok.at[own_end, chunks[c]]
+        return remote(ref, ref, t_send.at[1, c], t_recv.at[own_end, c], at(towards, lane))
+
+    def tok_wait(plane, c):
+        ref = tok.at[plane, chunks[c]]
+        remote(ref, ref, t_send.at[0, c], t_recv.at[plane, c], core_peer).wait_recv()
 
     weights_out(0)
-    own_out.start()
     weights_out(1)
+    own_out(0).start()
+    own_out(1).start()
     pick_in.wait()
 
     def pick_copy(step):
@@ -273,62 +285,77 @@
         for index in (2, 4, 6, 7, 8):
             gather_wait(kind, index)
 
-    def kv_rows(ref, plane, where):
-        return ref.at[pl.ds((plane * LANES + where) * nblk, nblk)]
-
-    def kv_copy(index, which, where, peer):
-        ref = kv_rows(kv, order[index], where)
-        return remote(ref, ref, k_send.at[which, index], k_recv.at[which, index], peer)
-
-    def kv_out(index):
-        kv_copy(index, 0, lane, y_peer).start()
-        kv_copy(index, 1, lane, core_peer).start()
-
-    def kv_forward(index):
-        kv_copy(index, 0, y_lane, y_peer).wait_recv()
-        kv_copy(index, 2, y_lane, core_peer).start()
-
-    def project(index, kind):
+    def kv_rows(ref, plane, where, first=0, count=nblk):
+        return ref.at[pl.ds((plane * LANES + where) * nblk + first, count)]
+
+    units = [(i, 0, ntok) for i in range(planes - 1)]
+    units += [(planes - 1, 0, chunk), (planes - 1, chunk, chunk)]
+
+    def unit_kv(unit, where):
+        index, first, count = units[unit]
+        return kv_rows(kv, order[index], where, first // BLOCK, count // BLOCK)
+
+    def unit_q(unit):
+        index, first, count = units[unit]
+        return qry.at[order[index], pl.ds(first, count)]
+
+    def kv_copy(unit, which, where, peer):
+        ref = unit_kv(unit, where)
+        return remote(ref, ref, k_send.at[which, unit], k_recv.at[which, unit], peer)
+
+    def kv_out(unit):
+        kv_copy(unit, 0, lane, y_peer).start()
+        kv_copy(unit, 1, lane, core_peer).start()
+
+    def kv_forward(unit):
+        kv_copy(unit, 0, y_lane, y_peer).wait_recv()
+        kv_copy(unit, 2, y_lane, core_peer).start()
+
+    def project(unit, kind):
+        index, first, count = units[unit]
         weights = wts[kind].reshape(-1, width)
-        res = jnp.dot(tok[order[index]], weights, preferred_element_type=jnp.float32)
-        return res.astype(jnp.bfloat16)
-
-    def far_copies(index):
-        p = order[index]
+        rows = tok[order[index], pl.ds(first, count)]
+        res = jnp.dot(rows, weights, preferred_element_type=jnp.float32).astype(jnp.bfloat16)
+        return res[:, :cols], res[:, cols:].reshape(count // BLOCK, BLOCK, 2 * cols)
+
+    def far_refs(unit):
+        index, first, count = units[unit]
+        blocks = pl.ds(index * nblk + first // BLOCK, count // BLOCK)
+        return far_q.at[index, pl.ds(first, count)], far_kv.at[blocks]
+
+    def far_copies(unit):
+        from_q, from_kv = far_refs(unit)
         return (
-            remote(far_q.at[index], qry.at[p], f_send.at[0, index], f_recv.at[0, index], at(mate, lane)),
-            remote(
-                far_kv.at[index], kv_rows(kv, p, lane), f_send.at[1, index], f_recv.at[1, index],
-                at(mate, lane),
-            ),
-        )
-
-    def project_far(index):
-        res = project(index, 0)
-        far_q[index] = res[:, :cols]
-        far_kv[index] = res[:, cols:].reshape(nblk, BLOCK, 2 * cols)
-        for copy in far_copies(index):
+            remote(from_kv, unit_kv(unit, lane), f_send.at[1, unit], f_recv.at[1, unit], at(mate, lane)),
+            remote(from_q, unit_q(unit), f_send.at[0, unit], f_recv.at[0, unit], at(mate, lane)),
+        )
+
+    def project_far(unit):
+        from_q, from_kv = far_refs(unit)
+        from_q[...], from_kv[...] = project(unit, 0)
+        for copy in far_copies(unit):
             copy.start()
 
-    def project_own(index):
-        res = project(index, 1)
-        qry[order[index]] = res[:, :cols]
-        kv_rows(kv, order[index], lane)[...] = res[:, cols:].reshape(nblk, BLOCK, 2 * cols)
-        kv_out(index)
+    def project_own(unit):
+        unit_q(unit)[...], unit_kv(unit, lane)[...] = project(unit, 1)
+        kv_out(unit)
 
     @pl.when(z == own_worker)
     def _():
         gather_first(0)
+        gather_second(0)
         tok_in.wait()
-        tok_wait(own_end)
-        pass_out.start()
-        gather_second(0)
+        tok_wait(own_end, 0)
+        pass_out(0).start()
         gather_first(1)
         gather_last(0)
         project_far(0)
+        tok_wait(own_end, 1)
+        pass_out(1).start()
         project_far(1)
         gather_second(1)
-        tok_wait(far_worker)
+        tok_wait(far_worker, 0)
+        tok_wait(far_worker, 1)
         project_far(2)
         gather_last(1)
         project_own(0)
@@ -336,23 +363,29 @@
         kv_forward(0)
         project_own(2)
         kv_forward(1)
-        tok_wait(far_end)
+        tok_wait(far_end, 0)
         project_far(3)
         project_own(3)
         kv_forward(2)
+        tok_wait(far_end, 1)
+        project_far(4)
+        project_own(4)
         kv_forward(3)
+        kv_forward(4)
 
     @pl.when(z != own_worker)
     def _():
         tok_in.wait()
-        for index in range(planes):
-            here_q, here_kv = qry.at[order[index]], kv_rows(kv, order[index], lane)
-            remote(here_kv, here_kv, f_send.at[1, index], f_recv.at[1, index], core_peer).wait_recv()
-            kv_out(index)
-            remote(here_q, here_q, f_send.at[0, index], f_recv.at[0, index], core_peer).wait_recv()
-            if index:
-                kv_forward(index - 1)
-        kv_forward(planes - 1)
+        for unit in range(len(units)):
+            here = unit_kv(unit, lane)
+            remote(here, here, f_send.at[1, unit], f_recv.at[1, unit], core_peer).wait_recv()
+            kv_out(unit)
+            if unit:
+                kv_forward(unit - 1)
+        kv_forward(len(units) - 1)
+        for unit in range(len(units)):
+            here = unit_q(unit)
+            remote(here, here, f_send.at[0, unit], f_recv.at[0, unit], core_peer).wait_recv()
 
     for step in range(1, planes):
         source = (z + step) % planes
@@ -367,15 +400,16 @@
     for index, (where, peer) in enumerate(partners):
         pick_lane(index, where, peer).wait_recv()
     glob = jnp.zeros((picks.shape[2], 2 * cols), jnp.float32)
-    for index in range(planes):
-        kv_copy(index, 1, core_lane, core_peer).wait_recv()
-        kv_copy(index, 2, diag_lane, core_peer).wait_recv()
+    for unit in range(len(units)):
+        kv_copy(unit, 1, core_lane, core_peer).wait_recv()
+        kv_copy(unit, 2, diag_lane, core_peer).wait_recv()
     for plane in range(planes):
         for where in range(LANES):
             rows = kv_rows(kv, plane, where)[...].reshape(ntok, 2 * cols)
             glob = glob + jnp.dot(picks[where, plane], rows, preferred_element_type=jnp.float32)
     glob = glob[: planes * LANES].astype(jnp.bfloat16)
-    blocks_in.wait()
+    dev_in.wait()
+    sub_in.wait()
     total_blocks = planes * LANES * nblk
     scale = HD ** (-0.5)
     keys = (3 + R) * BLOCK + glob.shape[0]
@@ -396,13 +430,12 @@
                 block,
                 jnp.minimum(block + 1, total_blocks - 1),
             ]
-            hidden = ((column < BLOCK) & (block == 0)) | (
-                (column >= 2 * BLOCK) & (column < 3 * BLOCK) & (block == total_blocks - 1)
-            )
             q_rows = slice(sub * BLOCK, (sub + 1) * BLOCK)
             for h in range(heads):
-                base = (block * H + z * heads + h) * R
-                where = starts + [blocks_ref[base + j] for j in range(R)]
+                head = z * heads + h
+                where = starts + [
+                    dev_ref[j, head, block] * nblk + sub_ref[j, head, block] for j in range(R)
+                ]
                 k_cols = slice(h * HD, (h + 1) * HD)
                 v_cols = slice(cols + h * HD, cols + (h + 1) * HD)
                 key = jnp.concatenate(
@@ -415,9 +448,13 @@
                     qry[plane, q_rows, k_cols], key, (((1,), (1,)), ((), ())),
                     preferred_element_type=jnp.float32,
                 ) * scale
-                score = jnp.where(hidden, -jnp.inf, score)
+                if sub == 0:
+                    score = jnp.where((column < BLOCK) & (block == 0), -jnp.inf, score)
+                if sub == nblk - 1:
+                    after = (column >= 2 * BLOCK) & (column < 3 * BLOCK)
+                    score = jnp.where(after & (block == total_blocks - 1), -jnp.inf, score)
                 expo = jnp.exp(score - jnp.max(score, axis=1, keepdims=True))
-                soft = (expo / jnp.sum(expo, axis=1, keepdims=True)).astype(jnp.bfloat16)
+                soft = (expo * (1.0 / jnp.sum(expo, axis=1, keepdims=True))).astype(jnp.bfloat16)
                 ctx[plane, q_rows, k_cols] = jnp.dot(
                     soft, val, preferred_element_type=jnp.float32
                 ).astype(jnp.bfloat16)
@@ -443,22 +480,24 @@
             for kind in range(2):
                 for part in range(3):
                     weight_remote(index, kind, part).wait_send()
-    own_out.wait_send()
+    for c in range(2):
+        own_out(c).wait_send()
 
     @pl.when(z == own_worker)
     def _():
-        pass_out.wait_send()
+        for c in range(2):
+            pass_out(c).wait_send()
         for kind in range(2):
             for index in range(len(moves)):
                 gather_out(kind, index).wait_send()
-        for index in range(planes):
-            for copy in far_copies(index):
+        for unit in range(len(units)):
+            for copy in far_copies(unit):
                 copy.wait_send()
 
-    for index in range(planes):
-        kv_copy(index, 0, lane, y_peer).wait_send()
-        kv_copy(index, 1, lane, core_peer).wait_send()
-        kv_copy(index, 2, y_lane, core_peer).wait_send()
+    for unit in range(len(units)):
+        kv_copy(unit, 0, lane, y_peer).wait_send()
+        kv_copy(unit, 1, lane, core_peer).wait_send()
+        kv_copy(unit, 2, y_lane, core_peer).wait_send()
     for step in range(1, planes):
         pick_copy(step).wait_send()
     for index, (where, peer) in enumerate(partners):
@@ -473,7 +512,7 @@
     picked = -(-nseq // 16) * 16
     cols = H // planes * HD
     half = w_query.shape[0] // 2
-    blocks = (rand_dev * nblk + rand_sub).reshape(-1)
+    dev, sub = rand_dev.transpose(2, 1, 0), rand_sub.transpose(2, 1, 0)
     shape = (picked, ntok)
     at_row = lax.broadcasted_iota(jnp.int32, shape, 0) == lax.axis_index("seq")
     at_event = lax.broadcasted_iota(jnp.int32, shape, 1) == global_off[0]
@@ -482,7 +521,7 @@
     return pl.pallas_call(
         functools.partial(fused_kernel, planes),
         out_shape=jax.ShapeDtypeStruct((ntok, H * HD), jnp.bfloat16),
-        in_specs=[pl.BlockSpec(memory_space=pl.ANY)] * 5,
+        in_specs=[pl.BlockSpec(memory_space=pl.ANY)] * 6,
         out_specs=pl.BlockSpec(memory_space=pl.ANY),
         scratch_shapes=[
             pltpu.VMEM((planes, ntok, width), jnp.bfloat16),
@@ -490,21 +529,22 @@
             pltpu.VMEM((planes, ntok, cols), jnp.bfloat16),
             pltpu.VMEM((nseq * nblk, BLOCK, 2 * cols), jnp.bfloat16),
             pltpu.VMEM((planes, ntok, cols), jnp.bfloat16),
-            pltpu.VMEM((planes, nblk, BLOCK, 2 * cols), jnp.bfloat16),
+            pltpu.VMEM((planes * nblk, BLOCK, 2 * cols), jnp.bfloat16),
             pltpu.VMEM((LANES, planes, picked, ntok), jnp.bfloat16),
             pltpu.VMEM((planes, ntok, cols), jnp.bfloat16),
-            pltpu.SMEM(blocks.shape, jnp.int32),
-            dma((3,)),
+            pltpu.SMEM(dev.shape, jnp.int32),
+            pltpu.SMEM(sub.shape, jnp.int32),
+            dma((4,)),
             dma((2, 2, 3)),
             dma((planes, 2, 3)),
             dma((2, 9)),
             dma((2, 9)),
-            dma((2,)),
-            dma((planes,)),
-            dma((2, planes)),
-            dma((2, planes)),
-            dma((3, planes)),
-            dma((3, planes)),
+            dma((2, 2)),
+            dma((planes, 2)),
+            dma((2, planes + 1)),
+            dma((2, planes + 1)),
+            dma((3, planes + 1)),
+            dma((3, planes + 1)),
             dma((planes - 1,)),
             dma((planes,)),
             dma((3,)),
@@ -513,14 +553,14 @@
             dma((planes,)),
         ],
         compiler_params=pltpu.CompilerParams(
-            collective_id=0, has_side_effects=True, vmem_limit_bytes=48 * 1024 * 1024
+            collective_id=0, has_side_effects=True, vmem_limit_bytes=60 * 1024 * 1024
         ),
         cost_estimate=pl.CostEstimate(
             flops=2 * planes * ntok * width * 3 * cols,
             bytes_accessed=2 * planes * ntok * width,
             transcendentals=ntok * H * 400,
         ),
-    )(tokens, w_query, w_keyval, pick, blocks)
+    )(tokens, w_query, w_keyval, pick, dev, sub)
 
 
 def solution(mesh):

time: 110 us -> 96.6 us (0.88); the launches traced: 108 us -> 96.4 us
  Pallas kernels: 103 us -> 93.2 us
  local copies, waits for them, and re-layouts: 3.35 us -> 1.87 us
    pallas_call x1, Pallas kernels: 103 us -> 93.2 us  [fused(): pl.pallas_call(functools.partial(fused_kernel, planes), out_shape=jax.Sha...]
    unnamed x9 -> x1, local copies, waits for them, and re-layouts: 2.97 us -> 1.87 us
where the time goes in v3:
time: 96.6 us; the launch traced here: 96.4 us
  Pallas kernels  93.2 us (96%)
  local copies, waits for them, and re-layouts  1.87 us (2%)
    pallas_call x1, Pallas kernels, fused(): pl.pallas_call(functools.partial(fused_kernel, planes), out_shape=jax.Sha...  93.2 us

profile of v3, /device:TPU:0, one launch (start us, length us, event | category | flops | bytes accessed | tf_op | source)
XLA Modules:
  0.0 96.4 jit_solution(6555248750167931020)
XLA Ops:
  0.7 0.7 select_convert_fusion.pick_hbm
  1.4 93.2 %shard_map.64 = bf16[256,1024]{1,0:T(8,128)(2,1)} custom-call(bf16[256,2048]{1,0:T(8,128)(2,1)} %tok_hbm.1, bf16[128,1024]{1,0:T(8,128)(2,1)} %wq_hbm.1, bf16[128,2048]{1,0:T(8,128)(2,1)} %wkv_hbm.1, bf16[16,256]{1,0:T(8,128)(2,1)} %select_convert_fusion.pick_hbm, s32[3,8,64]{2,1,0:T(8,128)} %bitcast.4, s32[3,8,64]{2,1,0:T(8,128)} %bitcast.5), custom_call_target="tpu_custom_call" | custom-call | flops 3221225472 | bytes 4194304 | tf_op jit(solution)/shard_map/pallas_call | solution.py:521
  94.6 1.9 %copy.9 = bf16[256,1024]{1,0:T(8,128)(2,1)} copy(bf16[256,1024]{1,0:T(8,128)(2,1)} %shard_map.64) | data formatting | bytes 1048576
  (2 shorter events, 0.0 us)

commit v4 on v3

--- a/solution.py
+++ b/solution.py
@@ -116,9 +116,14 @@
     return ctx.reshape(ntok, inner).astype(jnp.bfloat16)
 
 
+def chunks_of(ntok):
+    half, quarter = ntok // 2, ntok // 4
+    return ((0, half), (half, quarter), (half + quarter, quarter))
+
+
 def fused_kernel(
     planes, tok_hbm, wq_hbm, wkv_hbm, pick_hbm, dev_hbm, sub_hbm, out_ref,
-    tok, wts, qry, kv, far_q, far_kv, picks, ctx, dev_ref, sub_ref,
+    tok, wts, qry, kv, far_q, far_kv, picks, ctx, glob_sum, dev_ref, sub_ref,
     local_sem, w_send, w_recv, g_send, g_recv, t_send, t_recv, f_send, f_recv,
     k_send, k_recv, p_send, p_recv, o_send, o_recv, c_send, c_recv,
 ):
@@ -210,8 +215,8 @@
                 remote(here, here, w_send.at[0, kind, part], w_recv.at[plane, kind, part], core_peer).wait_recv()
 
     towards = jnp.where(lower, z + 1, z - 1)
-    chunk = ntok // 2
-    chunks = (pl.ds(0, chunk), pl.ds(chunk, chunk))
+    cuts = chunks_of(ntok)
+    chunks = [pl.ds(first, count) for first, count in cuts]
 
     def own_out(c):
         return remote(
@@ -229,13 +234,11 @@
 
     weights_out(0)
     weights_out(1)
-    own_out(0).start()
-    own_out(1).start()
-    pick_in.wait()
+    for c in range(len(cuts)):
+        own_out(c).start()
 
     def pick_copy(step):
-        ref = picks.at[lane, z]
-        return remote(ref, ref, p_send.at[step - 1], p_recv.at[z], at((z + step) % planes, lane))
+        return remote(pick_hbm, picks.at[lane, z], p_send.at[step - 1], p_recv.at[z], at((z + step) % planes, lane))
 
     for step in range(1, planes):
         pick_copy(step).start()
@@ -289,7 +292,7 @@
         return ref.at[pl.ds((plane * LANES + where) * nblk + first, count)]
 
     units = [(i, 0, ntok) for i in range(planes - 1)]
-    units += [(planes - 1, 0, chunk), (planes - 1, chunk, chunk)]
+    units += [(planes - 1, first, count) for first, count in cuts]
 
     def unit_kv(unit, where):
         index, first, count = units[unit]
@@ -339,6 +342,36 @@
     def project_own(unit):
         unit_q(unit)[...], unit_kv(unit, lane)[...] = project(unit, 1)
         kv_out(unit)
+
+    def pick_lane(index, where, peer):
+        return remote(picks.at[where], picks.at[where], o_send.at[index], o_recv.at[index], peer)
+
+    def picks_first():
+        pick_in.wait()
+        for step in range(1, planes):
+            source = (z + step) % planes
+            ref = picks.at[lane, source]
+            remote(ref, ref, p_send.at[0], p_recv.at[source], core_peer).wait_recv()
+        for index, (where, peer) in enumerate(partners):
+            pick_lane(index, lane, peer).start()
+
+    def picks_last():
+        for index, (where, peer) in enumerate(partners):
+            pick_lane(index, where, peer).wait_recv()
+
+    def glob_add(index):
+        for unit in [u for u in range(len(units)) if units[u][0] == index]:
+            kv_copy(unit, 1, core_lane, core_peer).wait_recv()
+            kv_copy(unit, 2, diag_lane, core_peer).wait_recv()
+        total = jnp.zeros(glob_sum.shape, jnp.float32) if index == 0 else glob_sum[...]
+        for where in range(LANES):
+            rows = kv_rows(kv, order[index], where)[...].reshape(ntok, 2 * cols)
+            total = total + jnp.dot(
+                picks[where, order[index]], rows, preferred_element_type=jnp.float32
+            )
+        glob_sum[...] = total
+
+    last = len(units) - 1
 
     @pl.when(z == own_worker)
     def _():
@@ -350,12 +383,14 @@
         gather_first(1)
         gather_last(0)
         project_far(0)
-        tok_wait(own_end, 1)
-        pass_out(1).start()
+        for c in range(1, len(cuts)):
+            tok_wait(own_end, c)
+            pass_out(c).start()
         project_far(1)
         gather_second(1)
-        tok_wait(far_worker, 0)
-        tok_wait(far_worker, 1)
+        picks_first()
+        for c in range(len(cuts)):
+            tok_wait(far_worker, c)
         project_far(2)
         gather_last(1)
         project_own(0)
@@ -363,51 +398,38 @@
         kv_forward(0)
         project_own(2)
         kv_forward(1)
-        tok_wait(far_end, 0)
-        project_far(3)
-        project_own(3)
-        kv_forward(2)
-        tok_wait(far_end, 1)
-        project_far(4)
-        project_own(4)
-        kv_forward(3)
-        kv_forward(4)
+        picks_last()
+        for unit in range(planes - 1, len(units)):
+            tok_wait(far_end, unit - planes + 1)
+            project_far(unit)
+            project_own(unit)
+            kv_forward(unit - 1)
+            if unit < last:
+                glob_add(unit - planes + 1)
+        glob_add(planes - 2)
+        kv_forward(last)
 
     @pl.when(z != own_worker)
     def _():
         tok_in.wait()
+        picks_first()
+        picks_last()
         for unit in range(len(units)):
             here = unit_kv(unit, lane)
             remote(here, here, f_send.at[1, unit], f_recv.at[1, unit], core_peer).wait_recv()
             kv_out(unit)
             if unit:
                 kv_forward(unit - 1)
-        kv_forward(len(units) - 1)
+            if planes - 1 <= unit < last:
+                glob_add(unit - planes + 1)
+        glob_add(planes - 2)
+        kv_forward(last)
         for unit in range(len(units)):
             here = unit_q(unit)
             remote(here, here, f_send.at[0, unit], f_recv.at[0, unit], core_peer).wait_recv()
 
-    for step in range(1, planes):
-        source = (z + step) % planes
-        ref = picks.at[lane, source]
-        remote(ref, ref, p_send.at[0], p_recv.at[source], core_peer).wait_recv()
-
-    def pick_lane(index, where, peer):
-        return remote(picks.at[where], picks.at[where], o_send.at[index], o_recv.at[index], peer)
-
-    for index, (where, peer) in enumerate(partners):
-        pick_lane(index, lane, peer).start()
-    for index, (where, peer) in enumerate(partners):
-        pick_lane(index, where, peer).wait_recv()
-    glob = jnp.zeros((picks.shape[2], 2 * cols), jnp.float32)
-    for unit in range(len(units)):
-        kv_copy(unit, 1, core_lane, core_peer).wait_recv()
-        kv_copy(unit, 2, diag_lane, core_peer).wait_recv()
-    for plane in range(planes):
-        for where in range(LANES):
-            rows = kv_rows(kv, plane, where)[...].reshape(ntok, 2 * cols)
-            glob = glob + jnp.dot(picks[where, plane], rows, preferred_element_type=jnp.float32)
-    glob = glob[: planes * LANES].astype(jnp.bfloat16)
+    glob_add(planes - 1)
+    glob = glob_sum[: planes * LANES].astype(jnp.bfloat16)
     dev_in.wait()
     sub_in.wait()
     total_blocks = planes * LANES * nblk
@@ -480,12 +502,12 @@
             for kind in range(2):
                 for part in range(3):
                     weight_remote(index, kind, part).wait_send()
-    for c in range(2):
+    for c in range(len(cuts)):
         own_out(c).wait_send()
 
     @pl.when(z == own_worker)
     def _():
-        for c in range(2):
+        for c in range(len(cuts)):
             pass_out(c).wait_send()
         for kind in range(2):
             for index in range(len(moves)):
@@ -518,6 +540,8 @@
     at_event = lax.broadcasted_iota(jnp.int32, shape, 1) == global_off[0]
     pick = jnp.where(at_row & at_event, 1.0, 0.0).astype(jnp.bfloat16)
     dma = pltpu.SemaphoreType.DMA
+    cuts = chunks_of(ntok)
+    units = planes - 1 + len(cuts)
     return pl.pallas_call(
         functools.partial(fused_kernel, planes),
         out_shape=jax.ShapeDtypeStruct((ntok, H * HD), jnp.bfloat16),
@@ -532,6 +556,7 @@
             pltpu.VMEM((planes * nblk, BLOCK, 2 * cols), jnp.bfloat16),
             pltpu.VMEM((LANES, planes, picked, ntok), jnp.bfloat16),
             pltpu.VMEM((planes, ntok, cols), jnp.bfloat16),
+            pltpu.VMEM((picked, 2 * cols), jnp.float32),
             pltpu.SMEM(dev.shape, jnp.int32),
             pltpu.SMEM(sub.shape, jnp.int32),
             dma((4,)),
@@ -539,12 +564,12 @@
             dma((planes, 2, 3)),
             dma((2, 9)),
             dma((2, 9)),
-            dma((2, 2)),
-            dma((planes, 2)),
-            dma((2, planes + 1)),
-            dma((2, planes + 1)),
-            dma((3, planes + 1)),
-            dma((3, planes + 1)),
+            dma((2, len(cuts))),
+            dma((planes, len(cuts))),
+            dma((2, units)),
+            dma((2, units)),
+            dma((3, units)),
+            dma((3, units)),
             dma((planes - 1,)),
             dma((planes,)),
             dma((3,)),

time: 96.6 us -> 94.7 us (0.980)
  Pallas kernels: 93.2 us -> 91.3 us
    pallas_call x1, Pallas kernels: 93.2 us -> 91.3 us  [fused(): pl.pallas_call(functools.partial(fused_kernel, planes), out_shape=jax.Sha...]
where the time goes in v4:
time: 94.7 us; the launch traced here: 94.5 us
  Pallas kernels  91.3 us (96%)
  local copies, waits for them, and re-layouts  1.87 us (2%)
    pallas_call x1, Pallas kernels, fused(): pl.pallas_call(functools.partial(fused_kernel, planes), out_shape=jax.Sha...  91.3 us

profile of v4, /device:TPU:0, one launch (start us, length us, event | category | flops | bytes accessed | tf_op | source)
XLA Modules:
  0.0 94.5 jit_solution(16421954878121935435)
XLA Ops:
  0.7 0.7 select_convert_fusion.pick_hbm
  1.4 91.3 %shard_map.64 = bf16[256,1024]{1,0:T(8,128)(2,1)} custom-call(bf16[256,2048]{1,0:T(8,128)(2,1)} %tok_hbm.1, bf16[128,1024]{1,0:T(8,128)(2,1)} %wq_hbm.1, bf16[128,2048]{1,0:T(8,128)(2,1)} %wkv_hbm.1, bf16[16,256]{1,0:T(8,128)(2,1)} %select_convert_fusion.pick_hbm, s32[3,8,64]{2,1,0:T(8,128)} %bitcast.4, s32[3,8,64]{2,1,0:T(8,128)} %bitcast.5), custom_call_target="tpu_custom_call" | custom-call | flops 3221225472 | bytes 4194304 | tf_op jit(solution)/shard_map/pallas_call | solution.py:545
  92.6 1.9 %copy.9 = bf16[256,1024]{1,0:T(8,128)(2,1)} copy(bf16[256,1024]{1,0:T(8,128)(2,1)} %shard_map.64) | data formatting | bytes 1048576
  (2 shorter events, 0.0 us)

commit v5 on v4

--- a/solution.py
+++ b/solution.py
@@ -1,4 +1,5 @@
 import functools
+import math
 
 import jax
 import jax.numpy as jnp
@@ -122,7 +123,7 @@
 
 
 def fused_kernel(
-    planes, tok_hbm, wq_hbm, wkv_hbm, pick_hbm, dev_hbm, sub_hbm, out_ref,
+    planes, tok_hbm, wq_hbm, wkv_hbm, off_ref, dev_hbm, sub_hbm, out_ref,
     tok, wts, qry, kv, far_q, far_kv, picks, ctx, glob_sum, dev_ref, sub_ref,
     local_sem, w_send, w_recv, g_send, g_recv, t_send, t_recv, f_send, f_recv,
     k_send, k_recv, p_send, p_recv, o_send, o_recv, c_send, c_recv,
@@ -166,10 +167,8 @@
 
     dev_in = pltpu.make_async_copy(dev_hbm, dev_ref, local_sem.at[0])
     dev_in.start()
-    sub_in = pltpu.make_async_copy(sub_hbm, sub_ref, local_sem.at[3])
+    sub_in = pltpu.make_async_copy(sub_hbm, sub_ref, local_sem.at[1])
     sub_in.start()
-    pick_in = pltpu.make_async_copy(pick_hbm, picks.at[lane, z], local_sem.at[1])
-    pick_in.start()
     tok_in = pltpu.make_async_copy(tok_hbm, tok.at[z], local_sem.at[2])
     tok_in.start()
 
@@ -234,11 +233,14 @@
 
     weights_out(0)
     weights_out(1)
-    for c in range(len(cuts)):
-        own_out(c).start()
+    own_out(0).start()
+
+    at_row = lax.broadcasted_iota(jnp.int32, picks.shape[2:], 0) == me
+    at_event = lax.broadcasted_iota(jnp.int32, picks.shape[2:], 1) == off_ref[0]
+    picks[lane, z] = jnp.where(at_row & at_event, 1.0, 0.0).astype(jnp.bfloat16)
 
     def pick_copy(step):
-        return remote(pick_hbm, picks.at[lane, z], p_send.at[step - 1], p_recv.at[z], at((z + step) % planes, lane))
+        return remote(picks.at[lane, z], picks.at[lane, z], p_send.at[step - 1], p_recv.at[z], at((z + step) % planes, lane))
 
     for step in range(1, planes):
         pick_copy(step).start()
@@ -347,7 +349,6 @@
         return remote(picks.at[where], picks.at[where], o_send.at[index], o_recv.at[index], peer)
 
     def picks_first():
-        pick_in.wait()
         for step in range(1, planes):
             source = (z + step) % planes
             ref = picks.at[lane, source]
@@ -376,7 +377,9 @@
     @pl.when(z == own_worker)
     def _():
         gather_first(0)
+        own_out(1).start()
         gather_second(0)
+        own_out(2).start()
         tok_in.wait()
         tok_wait(own_end, 0)
         pass_out(0).start()
@@ -411,6 +414,8 @@
 
     @pl.when(z != own_worker)
     def _():
+        own_out(1).start()
+        own_out(2).start()
         tok_in.wait()
         picks_first()
         picks_last()
@@ -433,7 +438,7 @@
     dev_in.wait()
     sub_in.wait()
     total_blocks = planes * LANES * nblk
-    scale = HD ** (-0.5)
+    scale = HD ** (-0.5) * math.log2(math.e)
     keys = (3 + R) * BLOCK + glob.shape[0]
     column = lax.broadcasted_iota(jnp.int32, (BLOCK, keys), 1)
 
@@ -469,13 +474,13 @@
                 score = lax.dot_general(
                     qry[plane, q_rows, k_cols], key, (((1,), (1,)), ((), ())),
                     preferred_element_type=jnp.float32,
-                ) * scale
+                )
                 if sub == 0:
                     score = jnp.where((column < BLOCK) & (block == 0), -jnp.inf, score)
                 if sub == nblk - 1:
                     after = (column >= 2 * BLOCK) & (column < 3 * BLOCK)
                     score = jnp.where(after & (block == total_blocks - 1), -jnp.inf, score)
-                expo = jnp.exp(score - jnp.max(score, axis=1, keepdims=True))
+                expo = jnp.exp2((score - jnp.max(score, axis=1, keepdims=True)) * scale)
                 soft = (expo * (1.0 / jnp.sum(expo, axis=1, keepdims=True))).astype(jnp.bfloat16)
                 ctx[plane, q_rows, k_cols] = jnp.dot(
                     soft, val, preferred_element_type=jnp.float32
@@ -535,17 +540,15 @@
     cols = H // planes * HD
     half = w_query.shape[0] // 2
     dev, sub = rand_dev.transpose(2, 1, 0), rand_sub.transpose(2, 1, 0)
-    shape = (picked, ntok)
-    at_row = lax.broadcasted_iota(jnp.int32, shape, 0) == lax.axis_index("seq")
-    at_event = lax.broadcasted_iota(jnp.int32, shape, 1) == global_off[0]
-    pick = jnp.where(at_row & at_event, 1.0, 0.0).astype(jnp.bfloat16)
     dma = pltpu.SemaphoreType.DMA
     cuts = chunks_of(ntok)
     units = planes - 1 + len(cuts)
     return pl.pallas_call(
         functools.partial(fused_kernel, planes),
         out_shape=jax.ShapeDtypeStruct((ntok, H * HD), jnp.bfloat16),
-        in_specs=[pl.BlockSpec(memory_space=pl.ANY)] * 6,
+        in_specs=[pl.BlockSpec(memory_space=pl.ANY)] * 3
+        + [pl.BlockSpec(memory_space=pltpu.SMEM)]
+        + [pl.BlockSpec(memory_space=pl.ANY)] * 2,
         out_specs=pl.BlockSpec(memory_space=pl.ANY),
         scratch_shapes=[
             pltpu.VMEM((planes, ntok, width), jnp.bfloat16),
@@ -559,7 +562,7 @@
             pltpu.VMEM((picked, 2 * cols), jnp.float32),
             pltpu.SMEM(dev.shape, jnp.int32),
             pltpu.SMEM(sub.shape, jnp.int32),
-            dma((4,)),
+            dma((3,)),
             dma((2, 2, 3)),
             dma((planes, 2, 3)),
             dma((2, 9)),
@@ -585,7 +588,7 @@
             bytes_accessed=2 * planes * ntok * width,
             transcendentals=ntok * H * 400,
         ),
-    )(tokens, w_query, w_keyval, pick, dev, sub)
+    )(tokens, w_query, w_keyval, global_off, dev, sub)
 
 
 def solution(mesh):

time: 94.7 us -> 94.5 us (level)
  no operation moved by 1% of the time
where the time goes in v5:
time: 94.5 us; the launch traced here: 94.4 us
  Pallas kernels  91.8 us (97%)
  local copies, waits for them, and re-layouts  1.87 us (2%)
    pallas_call x1, Pallas kernels, fused(): pl.pallas_call(functools.partial(fused_kernel, planes), out_shape=jax.Sha...  91.8 us

profile of v5, /device:TPU:0, one launch (start us, length us, event | category | flops | bytes accessed | tf_op | source)
XLA Modules:
  0.0 94.4 jit_solution(823230665629422887)
XLA Ops:
  0.7 91.8 %shard_map.64 = bf16[256,1024]{1,0:T(8,128)(2,1)} custom-call(bf16[256,2048]{1,0:T(8,128)(2,1)} %tok_hbm.1, bf16[128,1024]{1,0:T(8,128)(2,1)} %wq_hbm.1, bf16[128,2048]{1,0:T(8,128)(2,1)} %wkv_hbm.1, s32[1]{0:T(128)S(6)} %copy.8.off_ref, s32[3,8,64]{2,1,0:T(8,128)} %bitcast.2, s32[3,8,64]{2,1,0:T(8,128)} %bitcast.3), custom_call_target="tpu_custom_call" | custom-call | flops 3221225472 | bytes 4194304 | tf_op jit(solution)/shard_map/pallas_call | solution.py:546
  92.5 1.9 %copy.9 = bf16[256,1024]{1,0:T(8,128)(2,1)} copy(bf16[256,1024]{1,0:T(8,128)(2,1)} %shard_map.64) | data formatting | bytes 1048576

commit v6 on v5

--- a/solution.py
+++ b/solution.py
@@ -440,7 +440,7 @@
     total_blocks = planes * LANES * nblk
     scale = HD ** (-0.5) * math.log2(math.e)
     keys = (3 + R) * BLOCK + glob.shape[0]
-    column = lax.broadcasted_iota(jnp.int32, (BLOCK, keys), 1)
+    key_row = lax.broadcasted_iota(jnp.int32, (keys, heads * BLOCK), 0)
 
     def ctx_copy(plane, index):
         return remote(
@@ -458,33 +458,60 @@
                 jnp.minimum(block + 1, total_blocks - 1),
             ]
             q_rows = slice(sub * BLOCK, (sub + 1) * BLOCK)
+            picked = []
+            for j in range(R):
+                picked.append([
+                    dev_ref[j, z * heads + h, block] * nblk + sub_ref[j, z * heads + h, block]
+                    for h in range(heads)
+                ])
+
+            def side_by_side(first):
+                rows = [kv[w, :, first : first + cols] for w in starts]
+                for choice in picked:
+                    rows.append(jnp.concatenate(
+                        [
+                            kv[choice[h], :, first + h * HD : first + (h + 1) * HD]
+                            for h in range(heads)
+                        ],
+                        axis=1,
+                    ))
+                rows.append(glob[:, first : first + cols])
+                return jnp.concatenate(rows, axis=0)
+
+            queries = jnp.concatenate(
+                [
+                    jnp.concatenate(
+                        [
+                            qry[plane, q_rows, k * HD : (k + 1) * HD]
+                            if k == h
+                            else jnp.zeros((BLOCK, HD), jnp.bfloat16)
+                            for k in range(heads)
+                        ],
+                        axis=1,
+                    )
+                    for h in range(heads)
+                ],
+                axis=0,
+            )
+            score = lax.dot_general(
+                side_by_side(0), queries, (((1,), (1,)), ((), ())),
+                preferred_element_type=jnp.float32,
+            )
+            if sub == 0:
+                score = jnp.where((key_row < BLOCK) & (block == 0), -jnp.inf, score)
+            if sub == nblk - 1:
+                after = (key_row >= 2 * BLOCK) & (key_row < 3 * BLOCK)
+                score = jnp.where(after & (block == total_blocks - 1), -jnp.inf, score)
+            expo = jnp.exp2((score - jnp.max(score, axis=0, keepdims=True)) * scale)
+            soft = (expo * (1.0 / jnp.sum(expo, axis=0, keepdims=True))).astype(jnp.bfloat16)
+            res = lax.dot_general(
+                soft, side_by_side(cols), (((0,), (0,)), ((), ())),
+                preferred_element_type=jnp.float32,
+            ).astype(jnp.bfloat16)
             for h in range(heads):
-                head = z * heads + h
-                where = starts + [
-                    dev_ref[j, head, block] * nblk + sub_ref[j, head, block] for j in range(R)
+                ctx[plane, q_rows, h * HD : (h + 1) * HD] = res[
+                    h * BLOCK : (h + 1) * BLOCK, h * HD : (h + 1) * HD
                 ]
-                k_cols = slice(h * HD, (h + 1) * HD)
-                v_cols = slice(cols + h * HD, cols + (h + 1) * HD)
-                key = jnp.concatenate(
-                    [kv[w, :, k_cols] for w in where] + [glob[:, k_cols]], axis=0
-                )
-                val = jnp.concatenate(
-                    [kv[w, :, v_cols] for w in where] + [glob[:, v_cols]], axis=0
-                )
-                score = lax.dot_general(
-                    qry[plane, q_rows, k_cols], key, (((1,), (1,)), ((), ())),
-                    preferred_element_type=jnp.float32,
-                )
-                if sub == 0:
-                    score = jnp.where((column < BLOCK) & (block == 0), -jnp.inf, score)
-                if sub == nblk - 1:
-                    after = (column >= 2 * BLOCK) & (column < 3 * BLOCK)
-                    score = jnp.where(after & (block == total_blocks - 1), -jnp.inf, score)
-                expo = jnp.exp2((score - jnp.max(score, axis=1, keepdims=True)) * scale)
-                soft = (expo * (1.0 / jnp.sum(expo, axis=1, keepdims=True))).astype(jnp.bfloat16)
-                ctx[plane, q_rows, k_cols] = jnp.dot(
-                    soft, val, preferred_element_type=jnp.float32
-                ).astype(jnp.bfloat16)
 
     others = (far_end, far_worker, mate)
     for index, plane in enumerate(others):

time: 94.5 us -> 93.3 us (0.987)
  Pallas kernels: 91.8 us -> 90.5 us
    pallas_call x1, Pallas kernels: 91.8 us -> 90.5 us  [fused(): pl.pallas_call(functools.partial(fused_kernel, planes), out_shape=jax.Sha...]
where the time goes in v6:
time: 93.3 us; the launch traced here: 93.1 us
  Pallas kernels  90.5 us (97%)
  local copies, waits for them, and re-layouts  1.87 us (2%)
    pallas_call x1, Pallas kernels, fused(): pl.pallas_call(functools.partial(fused_kernel, planes), out_shape=jax.Sha...  90.5 us
    unnamed x1, local copies, waits for them, and re-layouts  1.87 us

profile of v6, /device:TPU:0, one launch (start us, length us, event | category | flops | bytes accessed | tf_op | source)
XLA Modules:
  0.0 93.1 jit_solution(712258745520573089)
XLA Ops:
  0.7 90.5 %shard_map.64 = bf16[256,1024]{1,0:T(8,128)(2,1)} custom-call(bf16[256,2048]{1,0:T(8,128)(2,1)} %tok_hbm.1, bf16[128,1024]{1,0:T(8,128)(2,1)} %wq_hbm.1, bf16[128,2048]{1,0:T(8,128)(2,1)} %wkv_hbm.1, s32[1]{0:T(128)S(6)} %copy.8.off_ref, s32[3,8,64]{2,1,0:T(8,128)} %bitcast.2, s32[3,8,64]{2,1,0:T(8,128)} %bitcast.3), custom_call_target="tpu_custom_call" | custom-call | flops 3221225472 | bytes 4194304 | tf_op jit(solution)/shard_map/pallas_call | solution.py:573
  91.2 1.9 %copy.9 = bf16[256,1024]{1,0:T(8,128)(2,1)} copy(bf16[256,1024]{1,0:T(8,128)(2,1)} %shard_map.64) | data formatting | bytes 1048576

commit v7 on v6

--- a/solution.py
+++ b/solution.py
@@ -338,8 +338,7 @@
     def project_far(unit):
         from_q, from_kv = far_refs(unit)
         from_q[...], from_kv[...] = project(unit, 0)
-        for copy in far_copies(unit):
-            copy.start()
+        far_copies(unit)[0].start()
 
     def project_own(unit):
         unit_q(unit)[...], unit_kv(unit, lane)[...] = project(unit, 1)
@@ -384,11 +383,13 @@
         tok_wait(own_end, 0)
         pass_out(0).start()
         gather_first(1)
+        tok_wait(own_end, 1)
+        pass_out(1).start()
         gather_last(0)
-        project_far(0)
-        for c in range(1, len(cuts)):
+        for c in range(2, len(cuts)):
             tok_wait(own_end, c)
             pass_out(c).start()
+        project_far(0)
         project_far(1)
         gather_second(1)
         picks_first()
@@ -405,6 +406,10 @@
         for unit in range(planes - 1, len(units)):
             tok_wait(far_end, unit - planes + 1)
             project_far(unit)
+            for earlier in range(unit + 1 if unit == planes - 1 else 0):
+                far_copies(earlier)[1].start()
+            if unit >= planes:
+                far_copies(unit)[1].start()
             project_own(unit)
             kv_forward(unit - 1)
             if unit < last:

time: 93.3 us -> 101 us (1.083); the launches traced: 93.1 us -> 99.7 us
  Pallas kernels: 90.5 us -> 97.2 us
    pallas_call x1, Pallas kernels: 90.5 us -> 97.2 us  [fused(): pl.pallas_call(functools.partial(fused_kernel, planes), out_shape=jax.Sha...]
where the time goes in v7:
time: 101 us; the launch traced here: 99.7 us
  Pallas kernels  97.2 us (96%)
  local copies, waits for them, and re-layouts  1.87 us (2%)
    pallas_call x1, Pallas kernels, fused(): pl.pallas_call(functools.partial(fused_kernel, planes), out_shape=jax.Sha...  97.2 us

profile of v7, /device:TPU:0, one launch (start us, length us, event | category | flops | bytes accessed | tf_op | source)
XLA Modules:
  0.0 99.7 jit_solution(7852914348554797537)
XLA Ops:
  0.7 97.2 %shard_map.64 = bf16[256,1024]{1,0:T(8,128)(2,1)} custom-call(bf16[256,2048]{1,0:T(8,128)(2,1)} %tok_hbm.1, bf16[128,1024]{1,0:T(8,128)(2,1)} %wq_hbm.1, bf16[128,2048]{1,0:T(8,128)(2,1)} %wkv_hbm.1, s32[1]{0:T(128)S(6)} %copy.8.off_ref, s32[3,8,64]{2,1,0:T(8,128)} %bitcast.2, s32[3,8,64]{2,1,0:T(8,128)} %bitcast.3), custom_call_target="tpu_custom_call" | custom-call | flops 3221225472 | bytes 4194304 | tf_op jit(solution)/shard_map/pallas_call | solution.py:578
  97.8 1.9 %copy.9 = bf16[256,1024]{1,0:T(8,128)(2,1)} copy(bf16[256,1024]{1,0:T(8,128)(2,1)} %shard_map.64) | data formatting | bytes 1048576

commit v8 on v6

--- a/solution.py
+++ b/solution.py
@@ -384,9 +384,11 @@
         tok_wait(own_end, 0)
         pass_out(0).start()
         gather_first(1)
+        tok_wait(own_end, 1)
+        pass_out(1).start()
         gather_last(0)
         project_far(0)
-        for c in range(1, len(cuts)):
+        for c in range(2, len(cuts)):
             tok_wait(own_end, c)
             pass_out(c).start()
         project_far(1)

time: 93.3 us -> 93.3 us (level)
  no operation moved by 1% of the time
where the time goes in v8:
time: 93.3 us; the launch traced here: 93.1 us
  Pallas kernels  90.5 us (97%)
  local copies, waits for them, and re-layouts  1.87 us (2%)
    pallas_call x1, Pallas kernels, fused(): pl.pallas_call(functools.partial(fused_kernel, planes), out_shape=jax.Sha...  90.5 us
    unnamed x1, local copies, waits for them, and re-layouts  1.87 us

profile of v8, /device:TPU:0, one launch (start us, length us, event | category | flops | bytes accessed | tf_op | source)
XLA Modules:
  0.0 93.1 jit_solution(7869171888186719322)
XLA Ops:
  0.7 90.5 %shard_map.64 = bf16[256,1024]{1,0:T(8,128)(2,1)} custom-call(bf16[256,2048]{1,0:T(8,128)(2,1)} %tok_hbm.1, bf16[128,1024]{1,0:T(8,128)(2,1)} %wq_hbm.1, bf16[128,2048]{1,0:T(8,128)(2,1)} %wkv_hbm.1, s32[1]{0:T(128)S(6)} %copy.8.off_ref, s32[3,8,64]{2,1,0:T(8,128)} %bitcast.2, s32[3,8,64]{2,1,0:T(8,128)} %bitcast.3), custom_call_target="tpu_custom_call" | custom-call | flops 3221225472 | bytes 4194304 | tf_op jit(solution)/shard_map/pallas_call | solution.py:575
  91.2 1.9 %copy.9 = bf16[256,1024]{1,0:T(8,128)(2,1)} copy(bf16[256,1024]{1,0:T(8,128)(2,1)} %shard_map.64) | data formatting | bytes 1048576
